TPU v7x, 32 devices: a whole 2x2x4 slice. The times are simulated.
32 devices in a mesh: batch: 32 (over z, y, x, core).
Axes of the slice: x: 2, y: 2, z: 4, core: 2. Of those that a mesh axis runs over, the one named last changes fastest.
Arguments:
- params: float32 [2473984], P('batch')
- moment1: float32 [2473984], P('batch')
- moment2: float32 [2473984], P('batch'), as said below
- ema_params: float32 [2473984], P('batch')
- trajectories: float32 [2, 64, 384, 6], P(None, 'batch'), may hold values from -6 to 6
- noise_draw: float32 [2, 64, 384, 6], P(None, 'batch'), may hold values from -6 to 6
- timesteps: int32 [2, 64], P(None, 'batch'), may hold values from 0 to 255
- lengths: int32 [2, 64], P(None, 'batch'), may hold values from 96 to 384, as said below
Outputs:
- new_params: float32 [2473984], P('batch')
- new_moment1: float32 [2473984], P('batch')
- new_moment2: float32 [2473984], P('batch')
- new_ema: float32 [2473984], P('batch')
- low_params: bfloat16 [2473984], P('batch')
- grad_norm: float32 [], replicated
- loss_sum: float32 [], replicated
- frame_count: float32 [], replicated
Inputs may be any that keep to these rules, and one draw needn't show every extreme that they name: `lengths`: in each micro-batch some horizon has all 384 frames valid. `moment2`: second moments are positive.
All inputs are finite; a program needn't handle non-finite values.
Results may differ from a plain program's by a relative error of at most 0.0068.
Values may be sent and summed in bfloat16 or wider, within the bound.
No kernel may reach another device: no remote copies, remote signals or barrier semaphores. Data moves between devices by JAX's collectives and lax.ppermute only.
A program may use at most 128 MiB of HBM per device.

v0:
```python
import math

import jax
import jax.numpy as jnp
from jax import lax
from jax.sharding import PartitionSpec as P

D = 256
TE = 128
CH = 6
GROUPS = 8
K = 5
DIFF = 256
STEP = 10


clip_limit = 0.05


def block_entries(entries, prefix, width_in, with_res):
    entries.append((prefix + "_conv1", K * width_in, D))
    entries.append((prefix + "_bias1", 1, D))
    entries.append((prefix + "_gain1", 1, D))
    entries.append((prefix + "_shift1", 1, D))
    entries.append((prefix + "_time", D, D))
    entries.append((prefix + "_time_bias", 1, D))
    entries.append((prefix + "_conv2", K * D, D))
    entries.append((prefix + "_bias2", 1, D))
    entries.append((prefix + "_gain2", 1, D))
    entries.append((prefix + "_shift2", 1, D))
    if with_res:
        entries.append((prefix + "_res", width_in, D))
        entries.append((prefix + "_res_bias", 1, D))


def layout():
    entries = [
        ("time_first", TE, D),
        ("time_first_bias", 1, D),
        ("time_second", D, D),
        ("time_second_bias", 1, D),
        ("input_conv", K * CH, D),
        ("input_bias", 1, D),
    ]
    block_entries(entries, "down", D, False)
    entries += [
        ("down_sample", 3 * D, D),
        ("down_sample_bias", 1, D),
        ("up_sample", 4 * D, D),
        ("up_sample_bias", 1, D),
    ]
    block_entries(entries, "up", 2 * D, True)
    entries += [("head", D, CH), ("head_bias", 1, CH)]
    return entries


def unpack(flat_weights):
    pieces = {}
    offset = 0
    for label, row_count, col_count in layout():
        piece = flat_weights[offset : offset + row_count * col_count]
        pieces[label] = piece.reshape(row_count, col_count) if row_count > 1 else piece
        offset += row_count * col_count
    return pieces


def rounded(values):
    return values.astype(jnp.bfloat16).astype(jnp.float32)


def mish(values):
    return values * jnp.tanh(jax.nn.softplus(values))


def product(values, weight):
    return jnp.einsum("...c,cd->...d", values, weight, preferred_element_type=jnp.float32)


def conv(values, weight, bias_row):
    tap_count = weight.shape[0] // values.shape[2]
    length = values.shape[1]
    padded = jnp.pad(values, ((0, 0), (tap_count // 2, tap_count // 2), (0, 0)))
    columns = jnp.concatenate(
        [padded[:, tap_index : tap_index + length] for tap_index in range(tap_count)], axis=2
    )
    return product(columns, weight) + bias_row


def group_norm(values, gain_row, shift_row):
    horizons, length, channels = values.shape
    grouped = values.reshape(horizons, length, GROUPS, channels // GROUPS)
    center = jnp.mean(grouped, axis=(1, 3), keepdims=True)
    spread = jnp.mean((grouped - center) ** 2, axis=(1, 3), keepdims=True)
    normed = ((grouped - center) * lax.rsqrt(spread + 1e-05)).reshape(horizons, length, channels)
    return normed * gain_row + shift_row


def res_block(values, timing, pieces, prefix, with_res):
    entered = rounded(values)
    hidden = mish(
        group_norm(
            conv(entered, pieces[prefix + "_conv1"], pieces[prefix + "_bias1"]),
            pieces[prefix + "_gain1"],
            pieces[prefix + "_shift1"],
        )
    )
    hidden = (
        hidden
        + (product(timing, pieces[prefix + "_time"]) + pieces[prefix + "_time_bias"])[:, None, :]
    )
    hidden = mish(
        group_norm(
            conv(rounded(hidden), pieces[prefix + "_conv2"], pieces[prefix + "_bias2"]),
            pieces[prefix + "_gain2"],
            pieces[prefix + "_shift2"],
        )
    )
    if with_res:
        return hidden + product(entered, pieces[prefix + "_res"]) + pieces[prefix + "_res_bias"]
    return hidden + values


def horizon_loss(flat_weights, trajectory, noise_part, diffusion_steps, lengths):
    pieces = unpack(flat_weights)
    horizons, length, channels = trajectory.shape
    frames = jnp.arange(length, dtype=jnp.int32)
    valid = (frames[None, :] < lengths[:, None]).astype(jnp.float32)
    times = diffusion_steps.astype(jnp.float32)
    angle_now = ((times + 1.0) / DIFF + 0.008) / 1.008 * (math.pi / 2)
    angle_zero = 0.008 / 1.008 * (math.pi / 2)
    share = jnp.cos(angle_now) ** 2 / math.cos(angle_zero) ** 2
    noisy = (
        jnp.sqrt(share)[:, None, None] * trajectory
        + jnp.sqrt(1.0 - share)[:, None, None] * noise_part
    ) * valid[:, :, None]
    half_width = TE // 2
    frequency = jnp.exp(
        -math.log(10000.0) * jnp.arange(half_width, dtype=jnp.float32) / (half_width - 1)
    )
    angles = times[:, None] * frequency[None, :]
    embedding = jnp.concatenate([jnp.sin(angles), jnp.cos(angles)], axis=1)
    timing = mish(product(rounded(embedding), pieces["time_first"]) + pieces["time_first_bias"])
    timing = product(rounded(timing), pieces["time_second"]) + pieces["time_second_bias"]
    timing = rounded(mish(timing))
    entry = conv(rounded(noisy), pieces["input_conv"], pieces["input_bias"])
    skipped = res_block(entry, timing, pieces, "down", False)
    padded = jnp.pad(rounded(skipped), ((0, 0), (1, 1), (0, 0)))
    columns = jnp.concatenate(
        [padded[:, 0:length:2], padded[:, 1 : length + 1 : 2], padded[:, 2 : length + 2 : 2]],
        axis=2,
    )
    coarse = product(columns, pieces["down_sample"]) + pieces["down_sample_bias"]
    half_len = length // 2
    lifted = jnp.pad(rounded(coarse), ((0, 0), (1, 1), (0, 0)))
    earlier, current, later = (
        lifted[:, 0:half_len],
        lifted[:, 1 : half_len + 1],
        lifted[:, 2 : half_len + 2],
    )
    kernel = pieces["up_sample"].reshape(4, D, D)
    even_rows = product(
        jnp.concatenate([current, earlier], axis=2), jnp.concatenate([kernel[1], kernel[3]], axis=0)
    )
    odd_rows = product(
        jnp.concatenate([later, current], axis=2), jnp.concatenate([kernel[0], kernel[2]], axis=0)
    )
    raised = (
        jnp.stack([even_rows, odd_rows], axis=2).reshape(horizons, length, D)
        + pieces["up_sample_bias"]
    )
    joined = jnp.concatenate([raised, skipped], axis=2)
    top = res_block(joined, timing, pieces, "up", True)
    prediction = product(rounded(top), pieces["head"]) + pieces["head_bias"]
    error = (prediction - noise_part) * valid[:, :, None]
    return jnp.sum(error * error)


def shards(params, moment1, moment2, ema_params, trajectories, noise_draw, timesteps, lengths):
    low_copy = params.astype(jnp.bfloat16)
    weights = lax.all_gather(low_copy, "batch", axis=0, tiled=True).astype(jnp.float32)
    local_sums = jnp.zeros_like(weights)
    local_loss = jnp.zeros((), jnp.float32)
    for portion in range(trajectories.shape[0]):
        portion_loss, pullback = jax.vjp(
            lambda flat_weights: horizon_loss(
                flat_weights,
                trajectories[portion],
                noise_draw[portion],
                timesteps[portion],
                lengths[portion],
            ),
            weights,
        )
        (gradient,) = pullback(jnp.ones((), jnp.float32))
        local_loss = local_loss + portion_loss
        local_sums = local_sums + gradient
    summed = lax.psum_scatter(local_sums, "batch", scatter_dimension=0, tiled=True)
    local_count = jnp.sum(lengths).astype(jnp.float32) * CH
    squares, loss_sum, frame_count = lax.psum(
        (jnp.sum(summed * summed), local_loss, local_count), "batch"
    )
    grad_norm = jnp.sqrt(squares) / frame_count
    clipped = summed / frame_count * jnp.minimum(1.0, clip_limit / (grad_norm + 1e-06))
    new_moment1 = 0.9 * moment1 + 0.1 * clipped
    new_moment2 = 0.95 * moment2 + 0.05 * clipped * clipped
    first_hat = new_moment1 / (1.0 - 0.9**STEP)
    second_hat = new_moment2 / (1.0 - 0.95**STEP)
    new_params = params - 0.01 * (first_hat / (jnp.sqrt(second_hat) + 1e-08) + 0.01 * params)
    new_ema = 0.8 * ema_params + 0.2 * new_params
    return (
        new_params,
        new_moment1,
        new_moment2,
        new_ema,
        new_params.astype(jnp.bfloat16),
        grad_norm,
        loss_sum,
        frame_count,
    )


def solution(mesh):
    placed = (
        P("batch"),
        P("batch"),
        P("batch"),
        P("batch"),
        P(None, "batch", None, None),
        P(None, "batch", None, None),
        P(None, "batch"),
        P(None, "batch"),
    )
    return jax.shard_map(
        shards,
        mesh=mesh,
        in_specs=placed,
        out_specs=(P("batch"), P("batch"), P("batch"), P("batch"), P("batch"), P(), P(), P()),
        check_vma=False,
    )
```

profile of v0, /device:TPU:0, one launch (start us, length us, event | category | flops | bytes accessed | tf_op | source)
XLA Modules:
  0.0 929.7 jit_solution(1300198491933232508)
XLA Ops:
  14.7 83.7 %all-gather.3.cloned.1.call-done = bf16[32,1,77312]{2,1,0:T(2,128)(2,1)} async-done(((bf16[1,1,77312]{2,1,0:T(2,128)(2,1)}), bf16[32,1,77312]{2,1,0:T(2,128)(2,1)}) %all-gather.3.cloned.1.call-update) | async-done | bytes 4947984 | tf_op jit(solution)/shard_map/all_gather | solution.py:180
  98.3 100.9 %reduce.84 = bf16[32,77312]{1,0:T(8,128)(2,1)} reduce(bf16[32,1,77312]{2,1,0:T(2,128)(2,1)} %all-gather.3.cloned.1.call-done, bf16[]{:T(256)} %constant.424), dimensions={1}, to_apply=%all-gather.reduce_sub_computation | reduce | bytes 9895938 | tf_op jit(solution)/shard_map/all_gather | solution.py:180
  199.3 9.8 %reshape.944 = bf16[2473984]{0:T(1024)(128)(2,1)} reshape(bf16[32,77312]{1,0:T(8,128)(2,1)} %reduce.84) | data formatting | bytes 9895936
  216.1 2.2 fusion.223
  220.9 2.7 slice.657
  223.7 3.0 fusion.222
  244.4 2.6 fusion.89
  259.1 3.6 reshape.951
  268.0 2.6 reshape.912
  293.7 1.9 fusion.96
  296.7 2.1 fusion.247
  304.2 1.8 multiply_reduce_fusion.20
  311.3 2.3 fusion.6
  322.8 1.8 multiply_reduce_fusion.8
  330.2 2.3 fusion.7
  334.4 4.0 multiply_reduce_fusion.7
  342.7 1.8 multiply_reduce_fusion.30
  360.4 1.8 multiply_reduce_fusion.38
  367.6 3.0 fusion.193
  370.7 1.8 convolution_bitcast_fusion.7
  374.0 1.8 convolution_bitcast_fusion.4
  377.6 4.8 multiply_reduce_fusion.17
  416.6 3.3 fusion.194
  419.9 2.8 convolution_bitcast_fusion.1
  425.4 2.0 fusion.249
  435.2 2.7 convolution_bitcast_fusion
  440.4 1.8 fusion.220
  442.2 2.0 fusion.248
  451.8 2.9 pad.689
  454.6 1.9 pad.688
  456.5 1.8 pad.1080
  459.4 2.7 pad.715
  462.2 2.8 pad.714
  464.9 1.8 pad.1079
  466.9 7.1 multiply_reduce_fusion.3
  475.9 2.5 fusion.196
  481.7 1.8 convolution_bitcast_fusion.3
  485.4 3.9 multiply_reduce_fusion.13
  501.7 1.8 convolution_bitcast_fusion.5
  503.4 2.6 fusion.258
  506.1 1.8 convolution_bitcast_fusion.2
  507.9 2.6 fusion.264
  518.2 2.8 copy.158
  544.2 2.4 fusion.227
  549.8 129.1 %add_add_fusion = f32[2473984]{0:T(1024)} fusion(f32[32768]{0:T(1024)S(1)} %bitcast.344, f32[256]{0:T(256)} %get-tuple-element.340, f32[65536]{0:T(1024)} %bitcast.342, f32[256]{0:T(256)} %get-tuple-element.342, f32[7680]{0:T(1024)} %reshape.940, f32[256]{0:T(256)} %get-tuple-element.138, f32[327680]{0:T(1024)} %bitcast.329, f32[256]{0:T(256)} %get-tuple-element.293, ...), kind=kLoop, calls=%fused_computation | loop fusion | flops 165756928 | bytes 29671472 | tf_op jit(solution)/shard_map/add | solution.py:196
  682.2 192.1 %all-reduce.146.cloned.1.call-done = f32[2473984]{0:T(1024)} async-done(((f32[2473984]{0:T(1024)}), f32[2473984]{0:T(1024)}) %all-reduce.146.cloned.1.call-update) | async-done | bytes 9895952
  876.0 40.2 %all-reduce.143 = (f32[]{:T(128)}, f32[]{:T(128)}, f32[]{:T(128)}) all-reduce(f32[]{:T(128)} %multiply_reduce_fusion.40, f32[]{:T(128)S(6)} %mul.1173, f32[]{:T(128)S(6)} %add.866), channel_id=1, replica_groups=mesh['batch'=32] {'batch'}, use_global_device_ids=true, to_apply=%region_130.133 | all-reduce | flops 3 | bytes 24 | tf_op jit(solution)/shard_map/psum | solution.py:199
  917.7 2.8 fusion.191
  (828 shorter events, 243.8 us)
Async XLA Ops:
  7.2 91.2 %all-gather.3.cloned.1.call-start = ((), (), s32[]{:S(2)}) async-start(), calls=%async_computation | async-start | bytes 10205184 | tf_op jit(solution)/shard_map/all_gather | solution.py:180
  9.1 865.1 %all-reduce.146.cloned.1.call-start = ((), (), s32[]{:S(2)}) async-start(), calls=%async_computation.1 | async-start | bytes 19791872
  10.9 188.3 %copy-start.149 = (f32[2,384]{1,0:T(2,128)}, f32[2,384]{1,0:T(2,128)S(1)}, u32[]{:S(2)}) copy-start(f32[2,384]{1,0:T(2,128)S(1)} %compare_convert_fusion) | copy-start | bytes 9220
  13.3 213.6 %copy-start.95 = (bf16[2,384,30]{1,2,0:T(8,128)(2,1)}, bf16[2,384,30]{1,2,0:T(8,128)(2,1)S(1)}, u32[]{:S(2)}) copy-start(bf16[2,384,30]{1,2,0:T(8,128)(2,1)S(1)} %concatenate.72) | copy-start | bytes 138244
  13.7 212.9 %copy-start.93 = (bf16[2,384,30]{1,2,0:T(8,128)(2,1)}, bf16[2,384,30]{1,2,0:T(8,128)(2,1)S(1)}, u32[]{:S(2)}) copy-start(bf16[2,384,30]{1,2,0:T(8,128)(2,1)S(1)} %concatenate.84) | copy-start | bytes 138244
  14.6 203.9 %copy-start.191 = (bf16[2,64]{1,0:T(2,128)(2,1)}, bf16[2,64]{1,0:T(2,128)(2,1)S(1)}, u32[]{:S(2)}) copy-start(bf16[2,64]{1,0:T(2,128)(2,1)S(1)} %get-tuple-element.313) | copy-start | bytes 772
  14.6 203.9 %copy-start.193 = (bf16[2,64]{1,0:T(2,128)(2,1)}, bf16[2,64]{1,0:T(2,128)(2,1)S(1)}, u32[]{:S(2)}) copy-start(bf16[2,64]{1,0:T(2,128)(2,1)S(1)} %get-tuple-element.314) | copy-start | bytes 772
  14.6 204.1 %copy-start.187 = (bf16[2,64]{1,0:T(2,128)(2,1)}, bf16[2,64]{1,0:T(2,128)(2,1)S(1)}, u32[]{:S(2)}) copy-start(bf16[2,64]{1,0:T(2,128)(2,1)S(1)} %get-tuple-element.307) | copy-start | bytes 772
  14.7 204.0 %copy-start.189 = (bf16[2,64]{1,0:T(2,128)(2,1)}, bf16[2,64]{1,0:T(2,128)(2,1)S(1)}, u32[]{:S(2)}) copy-start(bf16[2,64]{1,0:T(2,128)(2,1)S(1)} %get-tuple-element.308) | copy-start | bytes 772
  209.1 9.2 slice-start
  214.4 21.9 %copy-start.167 = (f32[256]{0:T(256)}, f32[256]{0:T(256)S(1)}, u32[]{:S(2)}) copy-start(f32[256]{0:T(256)S(1)} %get-tuple-element.172) | copy-start | bytes 3076
  214.4 21.9 %copy-start.171 = (f32[256]{0:T(256)}, f32[256]{0:T(256)S(1)}, u32[]{:S(2)}) copy-start(f32[256]{0:T(256)S(1)} %get-tuple-element.173) | copy-start | bytes 3076
  218.4 8.2 copy-start.39
  218.5 8.2 copy-start.37
  227.0 6.4 copy-start.9
  247.0 31.0 %copy-start.15 = (bf16[2,384,256]{2,1,0:T(8,128)(2,1)}, bf16[2,384,256]{2,1,0:T(8,128)(2,1)S(1)}, u32[]{:S(2)}) copy-start(bf16[2,384,256]{2,1,0:T(8,128)(2,1)S(1)} %get-tuple-element.290) | copy-start | bytes 1179652
  247.7 6.3 copy-start.76
  247.8 7.0 slice-start.1
  254.9 15.6 %copy-start.30 = (bf16[768,256,1]{1,0,2:T(8,128)(2,1)}, bf16[768,256,1]{1,0,2:T(8,128)(2,1)S(1)}, u32[]{:S(2)}) copy-start(bf16[768,256,1]{1,0,2:T(8,128)(2,1)S(1)} %reshape.948) | copy-start | bytes 1179652
  255.0 7.8 copy-start.45
  256.1 16.1 %copy-start.61 = (bf16[256,256]{1,0:T(8,128)(2,1)}, bf16[256,256]{1,0:T(8,128)(2,1)S(1)}, u32[]{:S(2)}) copy-start(bf16[256,256]{1,0:T(8,128)(2,1)S(1)} %slice.570) | copy-start | bytes 393220
  257.1 15.1 %copy-start.64 = (bf16[256,256]{1,0:T(8,128)(2,1)}, bf16[256,256]{1,0:T(8,128)(2,1)S(1)}, u32[]{:S(2)}) copy-start(bf16[256,256]{1,0:T(8,128)(2,1)S(1)} %slice.572) | copy-start | bytes 393220
  258.1 14.4 %copy-start.67 = (bf16[256,256]{1,0:T(8,128)(2,1)}, bf16[256,256]{1,0:T(8,128)(2,1)S(1)}, u32[]{:S(2)}) copy-start(bf16[256,256]{1,0:T(8,128)(2,1)S(1)} %slice.575) | copy-start | bytes 393220
  259.1 6.6 copy-start.70
  281.5 7.0 copy-start.19
  318.3 11.8 %copy-start.16 = (bf16[2,384,256]{2,1,0:T(8,128)(2,1)S(1)}, bf16[2,384,256]{2,1,0:T(8,128)(2,1)}, u32[]{:S(2)}) copy-start(bf16[2,384,256]{2,1,0:T(8,128)(2,1)} %copy-done.15) | copy-start | bytes 1179652
  459.4 7.4 copy-start.1
  459.4 7.4 copy-start.3
  459.4 7.4 copy-start.146
  466.8 7.3 copy-start.181
  466.8 7.5 copy-start.148
  466.8 8.4 copy-start.179
  466.8 9.0 copy-start.164
  466.8 9.0 copy-start.165
  466.8 9.0 copy-start.170
  485.3 9.4 %copy-start.183 = (f32[2,256]{1,0:T(2,128)S(1)}, f32[2,256]{1,0:T(2,128)}, u32[]{:S(2)}) copy-start(f32[2,256]{1,0:T(2,128)} %fusion.265) | copy-start | bytes 6148
  485.3 10.2 %copy-start.152 = (f32[2,256]{1,0:T(2,128)S(1)}, f32[2,256]{1,0:T(2,128)}, u32[]{:S(2)}) copy-start(f32[2,256]{1,0:T(2,128)} %copy-done.151) | copy-start | bytes 6148
  489.2 9.1 copy-start.175
  489.2 10.2 %copy-start.177 = (f32[2,8]{1,0:T(2,128)S(1)}, f32[2,8]{1,0:T(2,128)}, u32[]{:S(2)}) copy-start(f32[2,8]{1,0:T(2,128)} %copy-done.176) | copy-start | bytes 196
  528.1 7.0 copy-start.192
  528.1 7.0 copy-start.194
  528.1 7.4 copy-start.188
  528.1 7.4 copy-start.190
  533.4 6.5 copy-start.4
  678.9 238.8 %copy-start.59 = (f32[77312]{0:T(1024)S(1)}, f32[77312]{0:T(1024)}, u32[]{:S(2)}) copy-start(f32[77312]{0:T(1024)} %param.10) | copy-start | bytes 927748
  678.9 238.8 %copy-start.98 = (f32[77312]{0:T(1024)S(1)}, f32[77312]{0:T(1024)}, u32[]{:S(2)}) copy-start(f32[77312]{0:T(1024)} %param.11) | copy-start | bytes 927748
  678.9 238.7 %copy-start.99 = (f32[77312]{0:T(1024)S(1)}, f32[77312]{0:T(1024)}, u32[]{:S(2)}) copy-start(f32[77312]{0:T(1024)} %param.12) | copy-start | bytes 927748
  679.0 241.5 %copy-start.100 = (f32[77312]{0:T(1024)S(1)}, f32[77312]{0:T(1024)}, u32[]{:S(2)}) copy-start(f32[77312]{0:T(1024)} %param.13) | copy-start | bytes 927748
  (161 other events, 369.0 us)
Sparse Core Ops, SparseCore 0:
  11.5 86.8 all-gather.2
  679.1 195.1 all-reduce.145
where the time goes:
time: 941 us; the launch traced here: 930 us
  other arithmetic  323 us (34%)
  waiting for transfers between devices  276 us (29%)
  local copies, waits for them, and re-layouts  185 us (20%)
  matrix products  85 us (9%)
  blocking collectives  40.2 us (4%)
  between operations  21.4 us (2%)
    unnamed x3, waiting for transfers between devices  192 us
    add x1, other arithmetic, shards(): local_sums = local_sums + gradient  129 us
    all_gather x1, other arithmetic, shards(): lax.all_gather(low_copy, 'batch', axis=0, tiled=True).astype(jnp.float32)  101 us
    dot_general x80, matrix products, product(): jnp.einsum('...c,cd->...d', values, weight, preferred_element_type=jnp.fl...  85 us
    all_gather x1, waiting for transfers between devices, shards(): lax.all_gather(low_copy, 'batch', axis=0, tiled=True).astype(jnp.float32)  83.7 us
    unnamed x464, local copies, waits for them, and re-layouts  62.5 us
    psum x1, blocking collectives, shards(): lax.psum((jnp.sum(summed * summed), local_loss, local_count), 'batch')  40.2 us
    slice x24, local copies, waits for them, and re-layouts, unpack(): piece = flat_weights[offset:offset + row_count * col_count]  23.3 us
  transfers between devices with their start and end apart: 2, of which 2 were waited for; matrix products, arithmetic and copies ran while one was open for 1% of the time, Pallas kernels for 0%

commit v1 on v0

v1 whole, which is shorter than its diff:
```python
import math

import jax
import jax.numpy as jnp
from jax import lax
from jax.experimental import pallas as pl
from jax.experimental.pallas import tpu as pltpu
from jax.sharding import PartitionSpec as P

D = 256
TE = 128
CH = 6
GROUPS = 8
K = 5
DIFF = 256
STEP = 10

CHUNK = 64
HEAD = 8
clip_limit = 0.05

F32 = jnp.float32
BF16 = jnp.bfloat16


def block_entries(entries, prefix, width_in, with_res):
    entries.append((prefix + "_conv1", K * width_in))
    entries.append((prefix + "_bias1", 1))
    entries.append((prefix + "_gain1", 1))
    entries.append((prefix + "_shift1", 1))
    entries.append((prefix + "_time", D))
    entries.append((prefix + "_time_bias", 1))
    entries.append((prefix + "_conv2", K * D))
    entries.append((prefix + "_bias2", 1))
    entries.append((prefix + "_gain2", 1))
    entries.append((prefix + "_shift2", 1))
    if with_res:
        entries.append((prefix + "_res", width_in))
        entries.append((prefix + "_res_bias", 1))


def layout():
    entries = [
        ("time_first", TE),
        ("time_first_bias", 1),
        ("time_second", D),
        ("time_second_bias", 1),
        ("input_conv", K * CH),
        ("input_bias", 1),
    ]
    block_entries(entries, "down", D, False)
    entries += [
        ("down_sample", 3 * D),
        ("down_sample_bias", 1),
        ("up_sample", 4 * D),
        ("up_sample_bias", 1),
    ]
    block_entries(entries, "up", 2 * D, True)
    entries += [("head", CH), ("head_bias", 1)]
    rows = {}
    offset = 0
    for label, count in entries:
        rows[label] = (offset, count)
        offset += count
    return rows


ROWS = layout()
MATS = (
    "time_first",
    "time_second",
    "input_conv",
    "down_conv1",
    "down_time",
    "down_conv2",
    "down_sample",
    "up_sample",
    "up_conv1",
    "up_time",
    "up_conv2",
    "up_res",
)
SUMS = (
    "input_bias",
    "down_bias1",
    "down_gain1",
    "down_shift1",
    "down_bias2",
    "down_gain2",
    "down_shift2",
    "down_sample_bias",
    "up_sample_bias",
    "up_bias1",
    "up_gain1",
    "up_shift1",
    "up_bias2",
    "up_gain2",
    "up_shift2",
    "up_res_bias",
)
NORMS = ("down1", "down2", "up1", "up2")


def up_to(value, step):
    return -(-value // step) * step


def mm(left, right):
    return jnp.dot(left, right, preferred_element_type=F32)


def mm_nt(left, right):
    return lax.dot_general(left, right, (((1,), (1,)), ((), ())), preferred_element_type=F32)


def mm_tn(left, right):
    return lax.dot_general(left, right, (((0,), (0,)), ((), ())), preferred_element_type=F32)


def mish_pair(v):
    c = jnp.minimum(v, 20.0)
    e = jnp.exp(c)
    n = e * (e + 2.0)
    r = 1.0 / (n + 2.0)
    t = n * r
    return v * t, t + (4.0 * c) * (e * (1.0 + e)) * (r * r)


def fold(values):
    rows, cols = values.shape
    return jnp.sum(values.reshape(rows // 8, 8, cols), axis=0)


def pad_get(pad, start, size, stride=1):
    where = pl.ds(start, size, stride=stride) if stride > 1 else pl.ds(start, size)
    return jnp.concatenate([pad[0, where, :], pad[1, where, :]], axis=1)


def pad_set(pad, start, value, stride=1):
    size = value.shape[0]
    where = pl.ds(start, size, stride=stride) if stride > 1 else pl.ds(start, size)
    pad[0, where, :] = value[:, : D // 2]
    pad[1, where, :] = value[:, D // 2 :]


def group_sums(parts, ones):
    stacked = []
    for part in parts:
        high = part.astype(BF16).astype(F32)
        rest = part - high
        mid = rest.astype(BF16).astype(F32)
        stacked += [high, mid, rest - mid, jnp.zeros_like(part)]
    summed = mm(jnp.concatenate(stacked, axis=0).astype(BF16), ones)
    return [jnp.sum(summed[32 * i : 32 * i + 32], axis=0, keepdims=True) for i in range(len(parts))]


def make_kernel(n, shard_rows, pads, horizons, length):
    half = length // 2
    count_inv = 1.0 / (length * (D // GROUPS))
    blocks = n // 2
    total_rows = n * shard_rows
    pad_rows = sum(pads)
    rows_all = horizons * length
    halves_all = horizons * half
    chunks = [slice(i, i + CHUNK) for i in range(0, length, CHUNK)]

    def kernel(
        tab_a, tab_b, lens, xin, noise, emb,
        a0, a1, b0, b1,
        ga0, ga1, gb0, gb1, loss_out,
        stage, flat, ones, padA, padS, padR, padY, cols, cbuf, dbuf, rbuf,
        entry, topb, dy1, dy2, dy4, dyc, dent, xt,
        x_d1, x_d2, x_e, x_o, x_y, x_j, x_u2,
        xhat, mp, dskip, rstds, temb_d, temb_u, dtemb_d, dtemb_u, headT, dheadT, sums, hsum,
        w_tf, w_ts, w_in, w_d1, w_dt, w_d2, w_ds, w_us, w_u1, w_ut, w_u2, w_res,
        t_d1, t_d2, t_ds, t_us, t_u1, t_u2,
        sem,
    ):
        w = dict(zip(MATS, (w_tf, w_ts, w_in, w_d1, w_dt, w_d2, w_ds, w_us, w_u1, w_ut, w_u2, w_res)))

        def row(label):
            return flat[ROWS[label][0] : ROWS[label][0] + 1, :]

        def moves(refs_a, refs_b, inward):
            made = []
            for part, (refs, tab) in enumerate(((refs_a, tab_a), (refs_b, tab_b))):
                low = pads[0] * part
                for r in range(n):
                    far = refs[r // blocks].at[r % blocks]
                    near = stage.at[tab[r], pl.ds(low, pads[part]), :]
                    made.append(
                        pltpu.make_async_copy(far, near, sem) if inward else pltpu.make_async_copy(near, far, sem)
                    )
            return made

        inward = moves((a0, a1), (b0, b1), True)
        for move in inward:
            move.start()
        group_row = lax.broadcasted_iota(jnp.int32, (D, D), 0) // (D // GROUPS)
        group_col = lax.broadcasted_iota(jnp.int32, (D, D), 1) // (D // GROUPS)
        ones[...] = (group_row == group_col).astype(F32).astype(BF16)
        zero8 = jnp.zeros((8, D), F32)
        for pad, rows in ((padA, length), (padS, length), (padR, length), (padY, half)):
            pad_set(pad, 0, zero8)
            pad_set(pad, rows + 8, zero8)
        sums[...] = jnp.zeros_like(sums)
        dheadT[...] = jnp.zeros_like(dheadT)
        hsum[...] = jnp.zeros_like(hsum)
        loss_out[...] = jnp.zeros_like(loss_out)
        dtemb_d[...] = jnp.zeros_like(dtemb_d)
        dtemb_u[...] = jnp.zeros_like(dtemb_u)
        for move in inward:
            move.wait()

        for s in range(n):
            flat[s * shard_rows : s * shard_rows + pad_rows, :] = stage[s].astype(F32)
        for label in MATS:
            first, count = ROWS[label]
            count = up_to(count, 32)
            for i in range(0, count, CHUNK):
                size = min(CHUNK, count - i)
                w[label][i : i + size, :] = flat[first + i : first + i + size, :].astype(BF16)
        for source, target, taps in ((w_d1, t_d1, K), (w_d2, t_d2, K), (w_us, t_us, 4), (w_u2, t_u2, K)):
            for k in range(taps):
                target[k * D : k * D + D, :] = source[k * D : k * D + D, :].T
        for k, source in enumerate((0, 2, 1)):
            t_ds[k * D : k * D + D, :] = w_ds[source * D : source * D + D, :].T
        for k in range(K):
            for j in range(2):
                t_u1[k * D : k * D + D, j * D : j * D + D] = w_u1[(2 * k + j) * D : (2 * k + j + 1) * D, :].T
        for j in range(2):
            t_u1[K * D : K * D + D, j * D : j * D + D] = w_res[j * D : j * D + D, :].T

        first = ROWS["head"][0]
        head_rows = flat[first : first + 8, :].astype(BF16)
        at_row = lax.broadcasted_iota(jnp.int32, (D, D), 0)
        at_col = lax.broadcasted_iota(jnp.int32, (D, D), 1)
        sub_row = lax.broadcasted_iota(jnp.int32, (8, D), 0)
        sub_col = lax.broadcasted_iota(jnp.int32, (8, D), 1)
        headT[...] = jnp.zeros_like(headT)

        def picker(j):
            return ((at_col * CH + j) % D == at_row).astype(F32).astype(BF16)

        def picked(j):
            return (sub_col * CH + j) // D == sub_row

        for j in range(CH):
            spread = mm(head_rows, picker(j))
            headT[j : j + 1, :] = jnp.sum(jnp.where(picked(j), spread, 0.0), axis=0, keepdims=True)
        head_b = headT[...].astype(BF16)
        head_bias = row("head_bias")[:, :HEAD]
        head_bias = jnp.where(lax.broadcasted_iota(jnp.int32, (1, HEAD), 1) < CH, head_bias, 0.0)

        emb_b = emb[...]
        z1 = mm(emb_b, w_tf[...]) + row("time_first_bias")
        t1, slope1 = mish_pair(z1)
        t1 = t1.astype(BF16)
        z2 = mm(t1, w_ts[...]) + row("time_second_bias")
        t2, slope2 = mish_pair(z2)
        timing = t2.astype(BF16)
        temb_d[...] = mm(timing, w_dt[...]) + row("down_time_bias")
        temb_u[...] = mm(timing, w_ut[...]) + row("up_time_bias")

        def add_sum(label, value):
            i = SUMS.index(label)
            sums[i] = sums[i] + value

        def shifted(target, base, step, size, sign):
            for k in range(K):
                start = 8 + sign * (k - K // 2)
                for c in range(0, length, CHUNK):
                    target[pl.ds(base + c, CHUNK), step * k : step * k + D] = pad_get(padA, start + c, CHUNK).astype(BF16)

        def norm_forward(which, index, h, gain, shift, write):
            total = zero8
            for c in chunks:
                total = total + fold(cbuf[c, :])
            (mean,) = group_sums([total], ones[...])
            mean = mean * count_inv
            total = zero8
            for c in chunks:
                off = cbuf[c, :] - mean
                total = total + fold(off * off)
            (var,) = group_sums([total], ones[...])
            rstd = lax.rsqrt(var * count_inv + 1e-05)
            rstds[index, pl.ds(h, 1), :] = rstd
            for c in chunks:
                xh = (cbuf[c, :] - mean) * rstd
                value, slope = mish_pair(xh * gain + shift)
                xhat[which, c, :] = xh
                mp[which, c, :] = slope
                write(c, value)

        def norm_backward(which, index, h, prefix, number):
            gain = row(prefix + "_gain" + number)
            one = zero8
            two = zero8
            for c in chunks:
                dv = dbuf[c, :] * mp[which, c, :]
                one = one + fold(dv)
                two = two + fold(dv * xhat[which, c, :])
                dbuf[c, :] = dv
            add_sum(prefix + "_shift" + number, one)
            add_sum(prefix + "_gain" + number, two)
            mean1, mean2 = group_sums([one * gain, two * gain], ones[...])
            rstd = rstds[index, pl.ds(h, 1), :]
            scale = rstd * gain
            mean1 = rstd * (mean1 * count_inv)
            mean2 = rstd * (mean2 * count_inv)
            total = zero8
            for c in chunks:
                dc = dbuf[c, :] * scale - mean1 - xhat[which, c, :] * mean2
                pad_set(padA, c.start + 8, dc)
                total = total + fold(dc)
            add_sum(prefix + "_bias" + number, total)

        def rounded_to_dbuf(value):
            dbuf[...] = value.astype(BF16).astype(F32)

        def column_sum():
            total = zero8
            for c in chunks:
                total = total + fold(dbuf[c, :])
            return total

        @pl.loop(0, horizons)
        def _(h):
            base = pl.multiple_of(h * length, CHUNK)
            base2 = pl.multiple_of(h * half, CHUNK)
            rows = pl.ds(base, length)
            rows2 = pl.ds(base2, half)
            entry[...] = mm(xin[h], w_in[...]) + row("input_bias")
            for c in chunks:
                value = entry[c, :]
                pad_set(padA, c.start + 8, value)
                x_d1[pl.ds(base + c.start, CHUNK), :] = value.astype(BF16)
            shifted(cols, 0, D, K * D, 1)
            cbuf[...] = mm(cols[:, : K * D], w_d1[...]) + row("down_bias1")
            time_row = temb_d[pl.ds(h, 1), :]

            def write_d1(c, value):
                value = value + time_row
                pad_set(padA, c.start + 8, value)
                x_d2[pl.ds(base + c.start, CHUNK), :] = value.astype(BF16)

            norm_forward(2 + 2 * h, 0, h, row("down_gain1"), row("down_shift1"), write_d1)
            shifted(cols, 0, D, K * D, 1)
            cbuf[...] = mm(cols[:, : K * D], w_d2[...]) + row("down_bias2")

            def write_d2(c, value):
                pad_set(padS, c.start + 8, value + entry[c, :])

            norm_forward(3 + 2 * h, 1, h, row("down_gain2"), row("down_shift2"), write_d2)
            odd_before = pad_get(padS, 7, half, 2).astype(BF16)
            even = pad_get(padS, 8, half, 2).astype(BF16)
            odd = pad_get(padS, 9, half, 2).astype(BF16)
            x_e[rows2, :] = even
            x_o[rows2, :] = odd
            coarse = mm(jnp.concatenate([odd_before, even, odd], axis=1), w_ds[...]) + row("down_sample_bias")
            pad_set(padY, 8, coarse)
            now = coarse.astype(BF16)
            x_y[rows2, :] = now
            before = pad_get(padY, 7, half).astype(BF16)
            after = pad_get(padY, 9, half).astype(BF16)
            up_bias = row("up_sample_bias")
            pad_set(padR, 8, mm(now, w_us[D : 2 * D, :]) + mm(before, w_us[3 * D : 4 * D, :]) + up_bias, 2)
            pad_set(padR, 9, mm(after, w_us[0:D, :]) + mm(now, w_us[2 * D : 3 * D, :]) + up_bias, 2)
            for k in range(K):
                start = 8 + k - K // 2
                for c in chunks:
                    cols[c, 2 * k * D : 2 * k * D + D] = pad_get(padR, start + c.start, CHUNK).astype(BF16)
                    cols[c, 2 * k * D + D : 2 * k * D + 2 * D] = pad_get(padS, start + c.start, CHUNK).astype(BF16)
            middle = 2 * (K // 2) * D
            x_j[rows, :] = cols[:, middle : middle + 2 * D]
            rbuf[...] = mm(cols[:, middle : middle + 2 * D], w_res[...]) + row("up_res_bias")
            cbuf[...] = mm(cols[...], w_u1[...]) + row("up_bias1")
            time_up = temb_u[pl.ds(h, 1), :]

            def write_u1(c, value):
                value = value + time_up
                pad_set(padA, c.start + 8, value)
                x_u2[pl.ds(base + c.start, CHUNK), :] = value.astype(BF16)

            norm_forward(0, 2, h, row("up_gain1"), row("up_shift1"), write_u1)
            shifted(cols, 0, D, K * D, 1)
            cbuf[...] = mm(cols[:, : K * D], w_u2[...]) + row("up_bias2")

            def write_u2(c, value):
                topb[c, :] = (value + rbuf[c, :]).astype(BF16)

            norm_forward(1, 3, h, row("up_gain2"), row("up_shift2"), write_u2)
            prediction = mm_nt(topb[...], head_b) + head_bias
            frame = lax.broadcasted_iota(jnp.int32, (length, HEAD), 0)
            error = jnp.where(frame < lens[h], prediction - noise[h], 0.0)
            loss_out[...] = loss_out[...] + fold(error * error)
            error = 2.0 * error
            hsum[...] = hsum[...] + fold(error)
            error = error.astype(BF16)
            dheadT[...] = dheadT[...] + mm_tn(error, topb[...])
            dtop = mm(error, head_b).astype(BF16)
            dy1[rows, K * D : (K + 1) * D] = dtop
            dbuf[...] = dtop.astype(F32)
            add_sum("up_res_bias", column_sum())
            norm_backward(1, 3, h, "up", "2")
            shifted(dy2, base, D, K * D, -1)
            rounded_to_dbuf(mm(dy2[rows, :], t_u2[...]))
            dtemb_u[pl.ds(h, 1), :] = jnp.sum(column_sum(), axis=0, keepdims=True)
            norm_backward(0, 2, h, "up", "1")
            shifted(dy1, base, D, K * D, -1)
            dbuf[...] = mm(dy1[rows, :], t_u1[:, D:]).astype(BF16).astype(F32)
            pad_set(padR, 8, mm(dy1[rows, :], t_u1[:, :D]).astype(BF16).astype(F32))
            total = zero8
            for c in chunks:
                total = total + fold(pad_get(padR, c.start + 8, CHUNK))
            add_sum("up_sample_bias", total)
            dy4[rows2, 0:D] = pad_get(padR, 7, half, 2).astype(BF16)
            dy4[rows2, D : 2 * D] = pad_get(padR, 8, half, 2).astype(BF16)
            dy4[rows2, 2 * D : 3 * D] = pad_get(padR, 9, half, 2).astype(BF16)
            dy4[rows2, 3 * D : 4 * D] = pad_get(padR, 10, half, 2).astype(BF16)
            dcoarse = mm(dy4[rows2, :], t_us[...]).astype(BF16)
            dcoarse32 = dcoarse.astype(F32)
            pad_set(padY, 8, dcoarse32)
            add_sum("down_sample_bias", fold(dcoarse32))
            dyc[rows2, 0:D] = pad_get(padY, 9, half).astype(BF16)
            dyc[rows2, D : 2 * D] = dcoarse
            dodd = mm(dyc[rows2, :], t_ds[0 : 2 * D, :]).astype(BF16).astype(F32)
            deven = mm(dcoarse, t_ds[2 * D : 3 * D, :]).astype(BF16).astype(F32)
            pad_set(padA, 8, deven, 2)
            pad_set(padA, 9, dodd, 2)
            for c in chunks:
                dskip[h, c, :] = dbuf[c, :] + pad_get(padA, c.start + 8, CHUNK)

        def put(label, offset, value):
            first = ROWS[label][0] + offset
            flat[first : first + value.shape[0], :] = value

        def weight_grads(source, width, rows, dy, targets):
            for j in range(width // D):
                xt[j * D : j * D + D, 0:rows] = source[:, j * D : j * D + D].T
            for label, offset, block in targets:
                put(label, offset, mm(xt[0:width, 0:rows], dy[:, block * D : block * D + D]))

        weight_grads(
            x_j, 2 * D, rows_all, dy1, [("up_conv1", 2 * k * D, k) for k in range(K)] + [("up_res", 0, K)]
        )
        weight_grads(x_u2, D, rows_all, dy2, [("up_conv2", k * D, k) for k in range(K)])
        weight_grads(x_y, D, halves_all, dy4, [("up_sample", k * D, k) for k in range(4)])
        weight_grads(x_o, D, halves_all, dyc, [("down_sample", 0, 0), ("down_sample", 2 * D, 1)])
        weight_grads(x_e, D, halves_all, dyc, [("down_sample", D, 1)])

        @pl.loop(0, horizons)
        def _(h):
            base = pl.multiple_of(h * length, CHUNK)
            rows = pl.ds(base, length)
            dbuf[...] = dskip[h]
            norm_backward(3 + 2 * h, 1, h, "down", "2")
            shifted(dy2, base, D, K * D, -1)
            rounded_to_dbuf(mm(dy2[rows, :], t_d2[...]))
            dtemb_d[pl.ds(h, 1), :] = jnp.sum(column_sum(), axis=0, keepdims=True)
            norm_backward(2 + 2 * h, 0, h, "down", "1")
            shifted(dy1, base, D, K * D, -1)
            rounded_to_dbuf(mm(dy1[rows, : K * D], t_d1[...]))
            total = zero8
            for c in chunks:
                value = dbuf[c, :] + dskip[h, c, :]
                total = total + fold(value)
                dent[pl.ds(base + c.start, CHUNK), :] = value.astype(BF16)
            add_sum("input_bias", total)

        weight_grads(x_d2, D, rows_all, dy2, [("down_conv2", k * D, k) for k in range(K)])
        weight_grads(x_d1, D, rows_all, dy1, [("down_conv1", k * D, k) for k in range(K)])
        inputs = zero8
        for h in range(horizons):
            part = mm_tn(xin[h], dent[h * length : h * length + length, :])
            inputs = part if h == 0 else inputs + part
        put("input_conv", 0, inputs[: K * CH])

        down_b = dtemb_d[...].astype(BF16)
        up_b = dtemb_u[...].astype(BF16)
        put("down_time", 0, mm_tn(timing, down_b))
        put("up_time", 0, mm_tn(timing, up_b))
        dtiming = (mm_nt(down_b, w_dt[...]) + mm_nt(up_b, w_ut[...])).astype(BF16).astype(F32)
        dz2 = dtiming * slope2
        dz2_b = dz2.astype(BF16)
        put("time_second", 0, mm_tn(t1, dz2_b))
        dz1 = mm_nt(dz2_b, w_ts[...]).astype(BF16).astype(F32) * slope1
        put("time_first", 0, mm_tn(emb_b, dz1.astype(BF16)))
        for label, value in (
            ("time_first_bias", dz1),
            ("time_second_bias", dz2),
            ("down_time_bias", dtemb_d[...]),
            ("up_time_bias", dtemb_u[...]),
        ):
            put(label, 0, jnp.sum(value, axis=0, keepdims=True))
        for i, label in enumerate(SUMS):
            put(label, 0, jnp.sum(sums[i], axis=0, keepdims=True))

        tail = ROWS["head"][0]
        flat[tail : total_rows + 16, :] = jnp.zeros((total_rows + 16 - tail, D), F32)
        packed = jnp.zeros((8, D), F32)
        for j in range(CH):
            spread = jnp.where(picked(j), jnp.broadcast_to(dheadT[j : j + 1, :], (8, D)), 0.0)
            packed = packed + mm_nt(spread.astype(BF16), picker(j))
        put("head", 0, packed[:CH])
        first = ROWS["head_bias"][0]
        flat[first : first + 1, 0:HEAD] = jnp.sum(hsum[...], axis=0, keepdims=True)

        for s in range(n):
            stage[s] = flat[s * shard_rows : s * shard_rows + pad_rows, :].astype(BF16)
        outward = moves((ga0, ga1), (gb0, gb1), False)
        for move in outward:
            move.start()
        for move in outward:
            move.wait()

    vm = pltpu.VMEM
    scratch = [
        vm((n, pad_rows, D), BF16),
        vm((total_rows + pad_rows, D), F32),
        vm((D, D), BF16),
        vm((2, length + 16, D // 2), F32),
        vm((2, length + 16, D // 2), F32),
        vm((2, length + 16, D // 2), F32),
        vm((2, half + 16, D // 2), F32),
        vm((length, 2 * K * D), BF16),
        vm((length, D), F32),
        vm((length, D), F32),
        vm((length, D), F32),
        vm((length, D), F32),
        vm((length, D), BF16),
        vm((rows_all, (K + 1) * D), BF16),
        vm((rows_all, K * D), BF16),
        vm((halves_all, 4 * D), BF16),
        vm((halves_all, 2 * D), BF16),
        vm((rows_all, D), BF16),
        vm((2 * D, rows_all), BF16),
        vm((rows_all, D), BF16),
        vm((rows_all, D), BF16),
        vm((halves_all, D), BF16),
        vm((halves_all, D), BF16),
        vm((halves_all, D), BF16),
        vm((rows_all, 2 * D), BF16),
        vm((rows_all, D), BF16),
        vm((2 + 2 * horizons, length, D), F32),
        vm((2 + 2 * horizons, length, D), F32),
        vm((horizons, length, D), F32),
        vm((len(NORMS), 8, D), F32),
        vm((16, D), F32),
        vm((16, D), F32),
        vm((16, D), F32),
        vm((16, D), F32),
        vm((HEAD, D), F32),
        vm((HEAD, D), F32),
        vm((len(SUMS), 8, D), F32),
        vm((8, HEAD), F32),
    ]
    scratch += [vm((up_to(ROWS[label][1], 32), D), BF16) for label in MATS]
    scratch += [
        vm((K * D, D), BF16),
        vm((K * D, D), BF16),
        vm((3 * D, D), BF16),
        vm((4 * D, D), BF16),
        vm(((K + 1) * D, 2 * D), BF16),
        vm((K * D, D), BF16),
        pltpu.SemaphoreType.DMA,
    ]
    shapes = [
        jax.ShapeDtypeStruct((blocks, rows, D), BF16) for rows in (pads[0], pads[0], pads[1], pads[1])
    ] + [jax.ShapeDtypeStruct((8, HEAD), F32)]
    smem = pl.BlockSpec(memory_space=pltpu.SMEM)
    local = pl.BlockSpec(memory_space=pltpu.VMEM)
    remote = pl.BlockSpec(memory_space=pl.ANY)
    flops = 6 * 2100000 * rows_all
    return pl.pallas_call(
        kernel,
        out_shape=shapes,
        in_specs=[smem] * 3 + [local] * 3 + [remote] * 4,
        out_specs=[remote] * 4 + [local],
        scratch_shapes=scratch,
        compiler_params=pltpu.CompilerParams(vmem_limit_bytes=63 * 1024 * 1024),
        cost_estimate=pl.CostEstimate(flops=flops, bytes_accessed=10000000, transcendentals=3000000),
        name="train_step",
    )


def device_dims(n):
    known = {32: (4, 2, 2), 256: (4, 8, 4)}
    return known.get(n, (n // 2, 1, 1))


class Ring:
    def __init__(self, n):
        self.n = n
        self.dims = device_dims(n) + (2,)
        strides = [1]
        for size in self.dims[:0:-1]:
            strides.insert(0, strides[0] * size)
        self.strides = strides

    def moved(self, index, axis, step):
        at = index // self.strides[axis] % self.dims[axis]
        return index + ((at + step) % self.dims[axis] - at) * self.strides[axis]

    def send(self, values, axis, step):
        return lax.ppermute(values, "batch", [(i, self.moved(i, axis, step)) for i in range(self.n)])

    def table(self, me, order):
        result = jnp.zeros((1,), jnp.int32) + me
        for axis in order:
            result = jnp.stack([self.moved(result, axis, step) for step in range(self.dims[axis])], axis=1).reshape(-1)
        return result

    def gather(self, own, order):
        blocks = own[None]
        for axis in order[:0:-1]:
            size = self.dims[axis]
            arrived = [blocks] + [self.send(blocks, axis, size - step) for step in range(1, size)]
            blocks = jnp.concatenate(arrived, axis=0) if size > 1 else blocks
        axis = order[0]
        return blocks, self.send(blocks, axis, 1)

    def scatter(self, keep, away, order):
        terms = [keep, self.send(away, order[0], 1)]
        for axis in order[1:]:
            size = self.dims[axis]
            if size == 1:
                continue
            cut = [term.reshape((size, term.shape[0] // size) + term.shape[1:]) for term in terms]
            arrived = []
            for step in range(1, size):
                part = sum(term[step].astype(F32) for term in cut).astype(BF16)
                arrived.append(self.send(part, axis, step))
            terms = [term[0] for term in cut] + arrived
        return sum(term[0].astype(F32) for term in terms)

    def total(self, values):
        for axis in (3, 2, 1, 0):
            size = self.dims[axis]
            if size == 4:
                one, two, three = (self.send(values, axis, step) for step in (1, 2, 3))
                values = (values + two) + (one + three)
                continue
            while size > 1:
                size //= 2
                values = values + self.send(values, axis, size)
        return values


def prepare(trajectories, noise_draw, timesteps, lengths):
    horizons = trajectories.shape[0] * trajectories.shape[1]
    length = trajectories.shape[2]
    trajectory = trajectories.reshape(horizons, length, CH)
    noise_part = noise_draw.reshape(horizons, length, CH)
    lens = lengths.reshape(horizons)
    frames = jnp.arange(length, dtype=jnp.int32)
    valid = (frames[None, :] < lens[:, None]).astype(F32)
    times = timesteps.reshape(horizons).astype(F32)
    angle_now = ((times + 1.0) / DIFF + 0.008) / 1.008 * (math.pi / 2)
    angle_zero = 0.008 / 1.008 * (math.pi / 2)
    share = jnp.cos(angle_now) ** 2 / math.cos(angle_zero) ** 2
    noisy = (
        jnp.sqrt(share)[:, None, None] * trajectory + jnp.sqrt(1.0 - share)[:, None, None] * noise_part
    ) * valid[:, :, None]
    padded = jnp.pad(noisy.astype(BF16), ((0, 0), (K // 2, K // 2), (0, 0)))
    taps = [padded[:, k : k + length] for k in range(K)]
    taps.append(jnp.zeros((horizons, length, 32 - K * CH), BF16))
    xin = jnp.concatenate(taps, axis=2)
    half_width = TE // 2
    frequency = jnp.exp(-math.log(10000.0) * jnp.arange(half_width, dtype=F32) / (half_width - 1))
    angles = times[:, None] * frequency[None, :]
    embedding = jnp.concatenate([jnp.sin(angles), jnp.cos(angles)], axis=1).astype(BF16)
    embedding = jnp.pad(embedding, ((0, 16 - horizons), (0, 0)))
    noise8 = jnp.pad(noise_part, ((0, 0), (0, 0), (0, HEAD - CH)))
    return lens, xin, noise8, embedding


def solution(mesh):
    n = mesh.shape["batch"]

    def shards(params, moment1, moment2, ema_params, trajectories, noise_draw, timesteps, lengths):
        me = lax.axis_index("batch")
        ring = Ring(n)
        shard_rows = params.shape[0] // D
        pad_rows = up_to(shard_rows, 32)
        if pad_rows - shard_rows >= 16:
            pad_rows -= 16
        low_rows = up_to(pad_rows // 2, 16)
        pads = (low_rows, pad_rows - low_rows)
        order_a = (3, 2, 1, 0)
        order_b = (3, 1, 2, 0)
        low_copy = jnp.pad(params.astype(BF16).reshape(shard_rows, D), ((0, pad_rows - shard_rows), (0, 0)))
        a0, a1 = ring.gather(low_copy[:low_rows], order_a)
        b0, b1 = ring.gather(low_copy[low_rows:], order_b)
        lens, xin, noise8, embedding = prepare(trajectories, noise_draw, timesteps, lengths)
        horizons, length = noise8.shape[:2]
        call = make_kernel(n, shard_rows, pads, horizons, length)
        ga0, ga1, gb0, gb1, loss_parts = call(
            ring.table(me, order_a), ring.table(me, order_b), lens, xin, noise8, embedding, a0, a1, b0, b1
        )
        summed = jnp.concatenate([ring.scatter(ga0, ga1, order_a), ring.scatter(gb0, gb1, order_b)], axis=0)
        summed = summed[:shard_rows].reshape(-1)
        local_count = jnp.sum(lengths).astype(F32) * CH
        lane = jnp.arange(128)[None, :]
        loss_count = jnp.where(lane == 0, jnp.sum(loss_parts), jnp.where(lane == 1, local_count, 0.0))
        loss_count = ring.total(jnp.broadcast_to(loss_count, (8, 128)))
        loss_sum = loss_count[0, 0]
        frame_count = loss_count[0, 1]
        squares = ring.total(jnp.broadcast_to(jnp.sum(summed * summed), (8, 128)))[0, 0]
        grad_norm = jnp.sqrt(squares) / frame_count
        clipped = summed / frame_count * jnp.minimum(1.0, clip_limit / (grad_norm + 1e-06))
        new_moment1 = 0.9 * moment1 + 0.1 * clipped
        new_moment2 = 0.95 * moment2 + 0.05 * clipped * clipped
        first_hat = new_moment1 / (1.0 - 0.9**STEP)
        second_hat = new_moment2 / (1.0 - 0.95**STEP)
        new_params = params - 0.01 * (first_hat / (jnp.sqrt(second_hat) + 1e-08) + 0.01 * params)
        new_ema = 0.8 * ema_params + 0.2 * new_params
        return (
            new_params,
            new_moment1,
            new_moment2,
            new_ema,
            new_params.astype(BF16),
            grad_norm,
            loss_sum,
            frame_count,
        )

    flat = P("batch")
    wide = P(None, "batch", None, None)
    narrow = P(None, "batch")
    return jax.shard_map(
        shards,
        mesh=mesh,
        in_specs=(flat, flat, flat, flat, wide, wide, narrow, narrow),
        out_specs=(flat, flat, flat, flat, flat, P(), P(), P()),
        check_vma=False,
    )
```

time: 941 us -> 193 us (0.21); the launches traced: 930 us -> 193 us
  other arithmetic: 323 us -> 18.3 us
  waiting for transfers between devices: 276 us -> 47.6 us
  local copies, waits for them, and re-layouts: 185 us -> 16.6 us
  matrix products: 85 us -> 0 us
  Pallas kernels: 0 us -> 62.5 us
  starting transfers between devices: 0.08 us -> 43.5 us
  blocking collectives: 40.2 us -> 0 us
  between operations: 21.4 us -> 4.28 us
    unnamed x3 -> x0, waiting for transfers between devices: 192 us -> none
    add x1 -> x21, other arithmetic: 129 us -> 3.62 us  [the longest x2 2 us: scatter(): return sum((term[0].astype(F32) for term in terms))]
    all_gather x1 -> x0, other arithmetic: 101 us -> none  [shards(): lax.all_gather(low_copy, 'batch', axis=0, tiled=True).astype(jnp.float32)]
    dot_general x80 -> x0, matrix products: 85 us -> none  [product(): jnp.einsum('...c,cd->...d', values, weight, preferred_element_type=jnp.fl...]
    all_gather x1 -> x0, waiting for transfers between devices: 83.7 us -> none  [shards(): lax.all_gather(low_copy, 'batch', axis=0, tiled=True).astype(jnp.float32)]
    reduce_sum x72 -> x2, other arithmetic: 68.3 us -> 1.23 us  [the longest x1 0.63 us: shards(): local_count = jnp.sum(lengths).astype(F32) * CH]
    pallas_call x0 -> x1, Pallas kernels: none -> 62.5 us  [shards(): call(ring.table(me, order_a), ring.table(me, order_b), lens, xin, noise8,...]
    unnamed x464 -> x36, local copies, waits for them, and re-layouts: 62.5 us -> 5.77 us
  transfers between devices with their start and end apart: 2 -> 36, of which waited for: 2 -> 15; matrix products, arithmetic and copies ran while one was open for 1% -> 15% of each run, Pallas kernels for 0% -> 0%
where the time goes in v1:
time: 193 us
  Pallas kernels  62.5 us (32%)
  waiting for transfers between devices  47.6 us (25%)
  starting transfers between devices  43.5 us (23%)
  other arithmetic  18.3 us (9%)
  local copies, waits for them, and re-layouts  16.6 us (9%)
  between operations  4.28 us (2%)
    pallas_call x1, Pallas kernels, shards(): call(ring.table(me, order_a), ring.table(me, order_b), lens, xin, noise8,...  62.5 us
    ppermute x36, waiting for transfers between devices, send(): lax.ppermute(values, 'batch', [(i, self.moved(i, axis, step)) for i in ra...  47.6 us
    ppermute x36, starting transfers between devices, send(): lax.ppermute(values, 'batch', [(i, self.moved(i, axis, step)) for i in ra...  43.5 us
    convert_element_type x6, other arithmetic, scatter(): part = sum((term[step].astype(F32) for term in cut)).astype(BF16)  6.22 us
    unnamed x36, local copies, waits for them, and re-layouts  5.77 us
  transfers between devices with their start and end apart: 36, of which 15 were waited for; matrix products, arithmetic and copies ran while one was open for 15% of the time, Pallas kernels for 0%

profile of v1, /device:TPU:0, one launch (start us, length us, event | category | flops | bytes accessed | tf_op | source)
XLA Modules:
  0.0 192.8 jit_solution(8565216584614144451)
XLA Ops:
  0.6 1.0 convert_element_type.309
  1.7 5.1 %collective-permute-start.6 = (bf16[1,144,256]{2,1,0:T(8,128)(2,1)S(1)}, bf16[1,144,256]{2,1,0:T(8,128)(2,1)S(1)}, u32[]{:S(2)}, u32[]{:S(2)}) collective-permute-start(bf16[1,144,256]{2,1,0:T(8,128)(2,1)S(1)} %fusion.4), channel_id=1, source_target_pairs={{0,24},{1,25},{2,26},{3,27},{4,28},{5,29},{6,30},{7,31},{8,0},{9,1... | collective-permute-start | bytes 221192 | tf_op jit(solution)/shard_map/ppermute | solution.py:606
  6.8 1.0 collective-permute-start.8
  7.9 2.9 %collective-permute-start = (bf16[1,160,256]{2,1,0:T(8,128)(2,1)S(1)}, bf16[1,160,256]{2,1,0:T(8,128)(2,1)S(1)}, u32[]{:S(2)}, u32[]{:S(2)}) collective-permute-start(bf16[1,160,256]{2,1,0:T(8,128)(2,1)S(1)} %broadcast_in_dim.37), channel_id=1, source_target_pairs={{0,24},{1,25},{2,26},{3,27},{4,28},{5,29},{6,30},{7,31},{8,0},{9,1... | collective-permute-start | bytes 245768 | tf_op jit(solution)/shard_map/ppermute | solution.py:606
  10.7 1.1 collective-permute-start.1
  15.0 1.6 collective-permute-start.9
  18.4 2.5 %collective-permute-done.1 = bf16[1,160,256]{2,1,0:T(8,128)(2,1)S(1)} collective-permute-done((bf16[1,160,256]{2,1,0:T(8,128)(2,1)S(1)}, bf16[1,160,256]{2,1,0:T(8,128)(2,1)S(1)}, u32[]{:S(2)}, u32[]{:S(2)}) %collective-permute-start.1) | collective-permute-done | bytes 81952 | tf_op jit(solution)/shard_map/ppermute | solution.py:606
  20.9 1.6 collective-permute-start.3
  24.5 6.1 %collective-permute-done.3 = bf16[4,160,256]{2,1,0:T(8,128)(2,1)S(1)} collective-permute-done((bf16[4,160,256]{2,1,0:T(8,128)(2,1)S(1)}, bf16[4,160,256]{2,1,0:T(8,128)(2,1)S(1)}, u32[]{:S(2)}, u32[]{:S(2)}) %collective-permute-start.3) | collective-permute-done | bytes 327712 | tf_op jit(solution)/shard_map/ppermute | solution.py:606
  31.3 1.5 collective-permute-start.4
  33.6 1.5 collective-permute-start.10
  36.0 11.0 %collective-permute-done.4 = bf16[8,160,256]{2,1,0:T(8,128)(2,1)S(1)} collective-permute-done((bf16[8,160,256]{2,1,0:T(8,128)(2,1)S(1)}, bf16[8,160,256]{2,1,0:T(8,128)(2,1)S(1)}, u32[]{:S(2)}, u32[]{:S(2)}) %collective-permute-start.4) | collective-permute-done | bytes 655392 | tf_op jit(solution)/shard_map/ppermute | solution.py:606
  47.1 0.9 constant_dynamic-update-slice_fusion.5.a0
  48.0 0.9 constant_dynamic-update-slice_fusion.16.b0
  50.7 0.9 pad.17.noise
  52.6 2.0 %concatenate.32.xin = bf16[4,384,32]{2,1,0:T(8,128)(2,1)} concatenate(bf16[4,384,6]{2,1,0:T(8,128)(2,1)S(1)} %get-tuple-element.46, bf16[4,384,6]{2,1,0:T(8,128)(2,1)S(1)} %get-tuple-element.44, bf16[4,384,6]{2,1,0:T(8,128)(2,1)S(1)} %fusion.2, bf16[4,384,6]{2,1,0:T(8,128)(2,1)S(1)} %get-tuple-element.45, bf16[4,384,6]{2,1,0:T(8,128)(2,1)S(1)} %get-tuple-element.43, ...), dimensions={2} | concatenate | bytes 196608 | tf_op jit(solution)/shard_map/concatenate | solution.py:668
  55.4 62.5 %train_step.1 = (bf16[16,160,256]{2,1,0:T(8,128)(2,1)}, bf16[16,160,256]{2,1,0:T(8,128)(2,1)}, bf16[16,144,256]{2,1,0:T(8,128)(2,1)}, bf16[16,144,256]{2,1,0:T(8,128)(2,1)}, f32[8,8]{1,0:T(8,128)}) custom-call(s32[32]{0:T(128)} %reshape.1866.tab_a, s32[32]{0:T(128)} %reshape.1869.tab_b, s32[4]{0:T(128)} %copy-done.12, bf16[4,384,32]{2,1,0:T(8,128)(2,1)} %concatenate.32.xin, ...), custom_call_target="tpu_custom_call" | custom-call | flops 19353600000 | bytes 10000000 | tf_op jit(solution)/shard_map/train_step/pallas_call | solution.py:698
  118.5 2.5 %collective-permute-done.18 = bf16[16,144,256]{2,1,0:T(8,128)(2,1)S(1)} collective-permute-done((bf16[16,144,256]{2,1,0:T(8,128)(2,1)}, bf16[16,144,256]{2,1,0:T(8,128)(2,1)S(1)}, u32[]{:S(2)}, u32[]{:S(2)}) %collective-permute-start.18) | collective-permute-done | bytes 1179680 | tf_op jit(solution)/shard_map/ppermute | solution.py:606
  121.0 2.4 %add_convert_fusion.1 = bf16[8,144,256]{2,1,0:T(8,128)(2,1)} fusion(bf16[16,144,256]{2,1,0:T(8,128)(2,1)S(1)} %collective-permute-done.18, bf16[16,144,256]{2,1,0:T(8,128)(2,1)} %get-tuple-element.15), kind=kLoop, calls=%fused_computation.1 | loop fusion | flops 1179648 | bytes 1769472 | tf_op jit(solution)/shard_map/convert_element_type | solution.py:632
  123.4 1.5 collective-permute-start.19
  125.0 1.0 add_convert_fusion
  126.0 1.5 collective-permute-start.13
  130.1 9.0 %collective-permute-done.19 = bf16[8,144,256]{2,1,0:T(8,128)(2,1)} collective-permute-done((bf16[8,144,256]{2,1,0:T(8,128)(2,1)}, bf16[8,144,256]{2,1,0:T(8,128)(2,1)}, u32[]{:S(2)}, u32[]{:S(2)}) %collective-permute-start.19) | collective-permute-done | bytes 589856 | tf_op jit(solution)/shard_map/ppermute | solution.py:606
  139.1 1.2 add_convert_fusion.3
  140.4 1.6 collective-permute-start.20
  141.9 1.0 collective-permute-done.13
  143.7 1.2 collective-permute-start.25
  144.9 4.2 %collective-permute-done.20 = bf16[4,144,256]{2,1,0:T(8,128)(2,1)S(1)} collective-permute-done((bf16[4,144,256]{2,1,0:T(8,128)(2,1)S(1)}, bf16[4,144,256]{2,1,0:T(8,128)(2,1)S(1)}, u32[]{:S(2)}, u32[]{:S(2)}) %collective-permute-start.20) | collective-permute-done | bytes 294944 | tf_op jit(solution)/shard_map/ppermute | solution.py:606
  149.0 1.3 add_convert_fusion.9
  150.9 3.4 %collective-permute-start.23 = (bf16[1,144,256]{2,1,0:T(8,128)(2,1)S(1)}, bf16[1,144,256]{2,1,0:T(8,128)(2,1)S(1)}, u32[]{:S(2)}, u32[]{:S(2)}) collective-permute-start(bf16[1,144,256]{2,1,0:T(8,128)(2,1)S(1)} %get-tuple-element.41), channel_id=1, source_target_pairs={{0,24},{1,25},{2,26},{3,27},{4,28},{5,29},{6,30},{7,31},{8,0},{9,1... | collective-permute-start | bytes 221192 | tf_op jit(solution)/shard_map/ppermute | solution.py:606
  155.0 1.8 collective-permute-done.21
  156.8 2.7 %collective-permute-done.22 = bf16[1,144,256]{2,1,0:T(8,128)(2,1)S(1)} collective-permute-done((bf16[1,144,256]{2,1,0:T(8,128)(2,1)S(1)}, bf16[1,144,256]{2,1,0:T(8,128)(2,1)S(1)}, u32[]{:S(2)}, u32[]{:S(2)}) %collective-permute-start.22) | collective-permute-done | bytes 73760 | tf_op jit(solution)/shard_map/ppermute | solution.py:606
  159.4 2.5 %collective-permute-start.17 = (bf16[1,160,256]{2,1,0:T(8,128)(2,1)S(1)}, bf16[1,160,256]{2,1,0:T(8,128)(2,1)S(1)}, u32[]{:S(2)}, u32[]{:S(2)}) collective-permute-start(bf16[1,160,256]{2,1,0:T(8,128)(2,1)S(1)} %get-tuple-element.38), channel_id=1, source_target_pairs={{0,24},{1,25},{2,26},{3,27},{4,28},{5,29},{6,30},{7,31},{8,0},{9,1... | collective-permute-start | bytes 245768 | tf_op jit(solution)/shard_map/ppermute | solution.py:606
  162.0 1.0 add_bitcast_fusion.1
  163.1 2.0 %collective-permute-done.16 = bf16[1,160,256]{2,1,0:T(8,128)(2,1)S(1)} collective-permute-done((bf16[1,160,256]{2,1,0:T(8,128)(2,1)S(1)}, bf16[1,160,256]{2,1,0:T(8,128)(2,1)S(1)}, u32[]{:S(2)}, u32[]{:S(2)}) %collective-permute-start.16) | collective-permute-done | bytes 81952 | tf_op jit(solution)/shard_map/ppermute | solution.py:606
  165.0 1.0 add_bitcast_fusion
  167.5 1.1 collective-permute-start.26
  169.2 1.5 collective-permute-start.31
  171.6 3.2 %collective-permute-start.28 = (f32[8,128]{1,0:T(8,128)S(1)}, f32[8,128]{1,0:T(8,128)S(1)}, u32[]{:S(2)}, u32[]{:S(2)}) collective-permute-start(f32[8,128]{1,0:T(8,128)S(1)} %add.1037), channel_id=1, source_target_pairs={{0,8},{1,9},{2,10},{3,11},{4,12},{5,13},{6,14},{7,15},{8,16},{9,17... | collective-permute-start | bytes 12296 | tf_op jit(solution)/shard_map/ppermute | solution.py:606
  176.1 0.9 collective-permute-start.32
  177.0 1.4 collective-permute-done.29
  178.5 1.3 collective-permute-done.32
  179.8 0.9 collective-permute-start.33
  180.7 1.3 collective-permute-start.34
  181.9 2.5 %collective-permute-start.35 = (f32[8,128]{1,0:T(8,128)S(1)}, f32[8,128]{1,0:T(8,128)S(1)}, u32[]{:S(2)}, u32[]{:S(2)}) collective-permute-start(f32[8,128]{1,0:T(8,128)S(1)} %add.1043), channel_id=1, source_target_pairs={{0,24},{1,25},{2,26},{3,27},{4,28},{5,29},{6,30},{7,31},{8,0},{9,1... | collective-permute-start | bytes 12296 | tf_op jit(solution)/shard_map/ppermute | solution.py:606
  185.1 1.0 collective-permute-done.34
  188.8 2.0 %fusion.61 = (bf16[77312]{0:T(1024)(128)(2,1)}, f32[77312]{0:T(1024)S(1)}, f32[77312]{0:T(1024)}, f32[77312]{0:T(1024)}) fusion(f32[77312]{0:T(1024)S(1)} %copy-done.1, f32[77312]{0:T(1024)S(1)} %mul.306, f32[77312]{0:T(1024)S(1)} %copy-done.5, f32[77312]{0:T(1024)} %param.10), kind=kLoop, calls=%fused_computation.229 | loop fusion | flops 1236992 | bytes 2319360 | tf_op jit(solution)/shard_map/convert_element_type | solution.py:723
  190.8 0.8 multiply_add_fusion
  (142 shorter events, 23.5 us)
Async XLA Ops:
  0.6 13.4 %copy-start.10 = (s32[2,2]{1,0:T(2,128)S(1)}, s32[2,2]{1,0:T(2,128)}, u32[]{:S(2)}) copy-start(s32[2,2]{1,0:T(2,128)} %param.14) | copy-start | bytes 52
  1.7 12.5 %collective-permute-start.6 = (bf16[1,144,256]{2,1,0:T(8,128)(2,1)S(1)}, bf16[1,144,256]{2,1,0:T(8,128)(2,1)S(1)}, u32[]{:S(2)}, u32[]{:S(2)}) collective-permute-start(bf16[1,144,256]{2,1,0:T(8,128)(2,1)S(1)} %fusion.4), channel_id=1, source_target_pairs={{0,24},{1,25},{2,26},{3,27},{4,28},{5,29},{6,30},{7,31},{8,0},{9,1... | collective-permute-start | bytes 221192 | tf_op jit(solution)/shard_map/ppermute | solution.py:606
  6.8 8.1 %collective-permute-start.7 = (bf16[1,144,256]{2,1,0:T(8,128)(2,1)S(1)}, bf16[1,144,256]{2,1,0:T(8,128)(2,1)S(1)}, u32[]{:S(2)}, u32[]{:S(2)}) collective-permute-start(bf16[1,144,256]{2,1,0:T(8,128)(2,1)S(1)} %fusion.4), channel_id=1, source_target_pairs={{0,16},{1,17},{2,18},{3,19},{4,20},{5,21},{6,22},{7,23},{8,24},{9,... | collective-permute-start | bytes 221192 | tf_op jit(solution)/shard_map/ppermute | solution.py:606
  6.8 8.1 %collective-permute-start.8 = (bf16[1,144,256]{2,1,0:T(8,128)(2,1)S(1)}, bf16[1,144,256]{2,1,0:T(8,128)(2,1)S(1)}, u32[]{:S(2)}, u32[]{:S(2)}) collective-permute-start(bf16[1,144,256]{2,1,0:T(8,128)(2,1)S(1)} %fusion.4), channel_id=1, source_target_pairs={{0,8},{1,9},{2,10},{3,11},{4,12},{5,13},{6,14},{7,15},{8,16},{9,17... | collective-permute-start | bytes 221192 | tf_op jit(solution)/shard_map/ppermute | solution.py:606
  7.9 10.5 %collective-permute-start = (bf16[1,160,256]{2,1,0:T(8,128)(2,1)S(1)}, bf16[1,160,256]{2,1,0:T(8,128)(2,1)S(1)}, u32[]{:S(2)}, u32[]{:S(2)}) collective-permute-start(bf16[1,160,256]{2,1,0:T(8,128)(2,1)S(1)} %broadcast_in_dim.37), channel_id=1, source_target_pairs={{0,24},{1,25},{2,26},{3,27},{4,28},{5,29},{6,30},{7,31},{8,0},{9,1... | collective-permute-start | bytes 245768 | tf_op jit(solution)/shard_map/ppermute | solution.py:606
  10.7 10.1 %collective-permute-start.1 = (bf16[1,160,256]{2,1,0:T(8,128)(2,1)S(1)}, bf16[1,160,256]{2,1,0:T(8,128)(2,1)S(1)}, u32[]{:S(2)}, u32[]{:S(2)}) collective-permute-start(bf16[1,160,256]{2,1,0:T(8,128)(2,1)S(1)} %broadcast_in_dim.37), channel_id=1, source_target_pairs={{0,16},{1,17},{2,18},{3,19},{4,20},{5,21},{6,22},{7,23},{8,24},{9,... | collective-permute-start | bytes 245768 | tf_op jit(solution)/shard_map/ppermute | solution.py:606
  14.2 6.7 %collective-permute-start.2 = (bf16[1,160,256]{2,1,0:T(8,128)(2,1)S(1)}, bf16[1,160,256]{2,1,0:T(8,128)(2,1)S(1)}, u32[]{:S(2)}, u32[]{:S(2)}) collective-permute-start(bf16[1,160,256]{2,1,0:T(8,128)(2,1)S(1)} %broadcast_in_dim.37), channel_id=1, source_target_pairs={{0,8},{1,9},{2,10},{3,11},{4,12},{5,13},{6,14},{7,15},{8,16},{9,17... | collective-permute-start | bytes 245768 | tf_op jit(solution)/shard_map/ppermute | solution.py:606
  15.0 17.9 %collective-permute-start.9 = (bf16[4,144,256]{2,1,0:T(8,128)(2,1)S(1)}, bf16[4,144,256]{2,1,0:T(8,128)(2,1)S(1)}, u32[]{:S(2)}, u32[]{:S(2)}) collective-permute-start(bf16[4,144,256]{2,1,0:T(8,128)(2,1)S(1)} %pad_maximum_fusion.2), channel_id=1, source_target_pairs={{0,2},{1,3},{2,0},{3,1},{4,6},{5,7},{6,4},{7,5},{8,10},{9,11},{10,... | collective-permute-start | bytes 884744 | tf_op jit(solution)/shard_map/ppermute | solution.py:606
  20.9 9.6 %collective-permute-start.3 = (bf16[4,160,256]{2,1,0:T(8,128)(2,1)S(1)}, bf16[4,160,256]{2,1,0:T(8,128)(2,1)S(1)}, u32[]{:S(2)}, u32[]{:S(2)}) collective-permute-start(bf16[4,160,256]{2,1,0:T(8,128)(2,1)S(1)} %pad_maximum_fusion), channel_id=1, source_target_pairs={{0,4},{1,5},{2,6},{3,7},{4,0},{5,1},{6,2},{7,3},{8,12},{9,13},{10,... | collective-permute-start | bytes 983048 | tf_op jit(solution)/shard_map/ppermute | solution.py:606
  31.3 15.7 %collective-permute-start.4 = (bf16[8,160,256]{2,1,0:T(8,128)(2,1)S(1)}, bf16[8,160,256]{2,1,0:T(8,128)(2,1)S(1)}, u32[]{:S(2)}, u32[]{:S(2)}) collective-permute-start(bf16[8,160,256]{2,1,0:T(8,128)(2,1)S(1)} %get-tuple-element.47), channel_id=1, source_target_pairs={{0,2},{1,3},{2,0},{3,1},{4,6},{5,7},{6,4},{7,5},{8,10},{9,11},{10,... | collective-permute-start | bytes 1966088 | tf_op jit(solution)/shard_map/ppermute | solution.py:606
  33.6 16.4 %copy-start.7 = (f32[2,2,384,6]{2,1,3,0:T(2,128)S(1)}, f32[2,2,384,6]{2,1,3,0:T(2,128)}, u32[]{:S(2)}) copy-start(f32[2,2,384,6]{2,1,3,0:T(2,128)} %param.13) | copy-start | bytes 110596
  33.6 14.4 %collective-permute-start.10 = (bf16[8,144,256]{2,1,0:T(8,128)(2,1)S(1)}, bf16[8,144,256]{2,1,0:T(8,128)(2,1)S(1)}, u32[]{:S(2)}, u32[]{:S(2)}) collective-permute-start(bf16[8,144,256]{2,1,0:T(8,128)(2,1)S(1)} %get-tuple-element.49), channel_id=1, source_target_pairs={{0,4},{1,5},{2,6},{3,7},{4,0},{5,1},{6,2},{7,3},{8,12},{9,13},{10,... | collective-permute-start | bytes 1769480 | tf_op jit(solution)/shard_map/ppermute | solution.py:606
  48.0 2.4 %copy-start.11 = (s32[2,2]{1,0:T(2,128)S(1)}, s32[2,2]{1,0:T(2,128)}, u32[]{:S(2)}) copy-start(s32[2,2]{1,0:T(2,128)} %param.15) | copy-start | bytes 52
  48.0 2.5 %copy-start.8 = (f32[2,2,384,6]{2,1,3,0:T(2,128)S(1)}, f32[2,2,384,6]{2,1,3,0:T(2,128)}, u32[]{:S(2)}) copy-start(f32[2,2,384,6]{2,1,3,0:T(2,128)} %param.12) | copy-start | bytes 110596
  48.0 7.4 %collective-permute-start.5 = (bf16[16,160,256]{2,1,0:T(8,128)(2,1)}, bf16[16,160,256]{2,1,0:T(8,128)(2,1)}, u32[]{:S(2)}, u32[]{:S(2)}) collective-permute-start(bf16[16,160,256]{2,1,0:T(8,128)(2,1)} %constant_dynamic-update-slice_fusion.5.a0), channel_id=1, source_target_pairs={{0,1},{1,0},{2,3},{3,2},{4,5},{5,4},{6,7},{7,6},{8,9},{9,8},{10,11... | collective-permute-start | bytes 3932168 | tf_op jit(solution)/shard_map/ppermute | solution.py:606
  48.8 6.5 %collective-permute-start.11 = (bf16[16,144,256]{2,1,0:T(8,128)(2,1)}, bf16[16,144,256]{2,1,0:T(8,128)(2,1)}, u32[]{:S(2)}, u32[]{:S(2)}) collective-permute-start(bf16[16,144,256]{2,1,0:T(8,128)(2,1)} %constant_dynamic-update-slice_fusion.16.b0), channel_id=1, source_target_pairs={{0,1},{1,0},{2,3},{3,2},{4,5},{5,4},{6,7},{7,6},{8,9},{9,8},{10,11... | collective-permute-start | bytes 3538952 | tf_op jit(solution)/shard_map/ppermute | solution.py:606
  50.4 1.6 copy-start.12
  117.9 7.1 %copy-start = (bf16[16,160,256]{2,1,0:T(8,128)(2,1)S(1)}, bf16[16,160,256]{2,1,0:T(8,128)(2,1)}, u32[]{:S(2)}) copy-start(bf16[16,160,256]{2,1,0:T(8,128)(2,1)} %get-tuple-element.13) | copy-start | bytes 3932164
  117.9 3.1 %collective-permute-start.18 = (bf16[16,144,256]{2,1,0:T(8,128)(2,1)}, bf16[16,144,256]{2,1,0:T(8,128)(2,1)S(1)}, u32[]{:S(2)}, u32[]{:S(2)}) collective-permute-start(bf16[16,144,256]{2,1,0:T(8,128)(2,1)} %get-tuple-element.16), channel_id=1, source_target_pairs={{0,1},{1,0},{2,3},{3,2},{4,5},{5,4},{6,7},{7,6},{8,9},{9,8},{10,11... | collective-permute-start | bytes 3538952 | tf_op jit(solution)/shard_map/ppermute | solution.py:606
  118.0 7.0 %collective-permute-start.12 = (bf16[16,160,256]{2,1,0:T(8,128)(2,1)}, bf16[16,160,256]{2,1,0:T(8,128)(2,1)S(1)}, u32[]{:S(2)}, u32[]{:S(2)}) collective-permute-start(bf16[16,160,256]{2,1,0:T(8,128)(2,1)} %get-tuple-element.14), channel_id=1, source_target_pairs={{0,1},{1,0},{2,3},{3,2},{4,5},{5,4},{6,7},{7,6},{8,9},{9,8},{10,11... | collective-permute-start | bytes 3932168 | tf_op jit(solution)/shard_map/ppermute | solution.py:606
  121.0 4.0 %copy-start.3 = (bf16[16,144,256]{2,1,0:T(8,128)(2,1)}, bf16[16,144,256]{2,1,0:T(8,128)(2,1)S(1)}, u32[]{:S(2)}) copy-start(bf16[16,144,256]{2,1,0:T(8,128)(2,1)S(1)} %collective-permute-done.18) | copy-start | bytes 3538948
  123.4 5.3 %copy-start.9 = (f32[8,8]{1,0:T(8,128)S(1)}, f32[8,8]{1,0:T(8,128)}, u32[]{:S(2)}) copy-start(f32[8,8]{1,0:T(8,128)} %get-tuple-element.17) | copy-start | bytes 772
  123.4 15.7 %collective-permute-start.19 = (bf16[8,144,256]{2,1,0:T(8,128)(2,1)}, bf16[8,144,256]{2,1,0:T(8,128)(2,1)}, u32[]{:S(2)}, u32[]{:S(2)}) collective-permute-start(bf16[8,144,256]{2,1,0:T(8,128)(2,1)} %add_convert_fusion.1), channel_id=1, source_target_pairs={{0,4},{1,5},{2,6},{3,7},{4,0},{5,1},{6,2},{7,3},{8,12},{9,13},{10,... | collective-permute-start | bytes 1769480 | tf_op jit(solution)/shard_map/ppermute | solution.py:606
  126.0 17.0 %collective-permute-start.13 = (bf16[8,160,256]{2,1,0:T(8,128)(2,1)}, bf16[8,160,256]{2,1,0:T(8,128)(2,1)S(1)}, u32[]{:S(2)}, u32[]{:S(2)}) collective-permute-start(bf16[8,160,256]{2,1,0:T(8,128)(2,1)} %add_convert_fusion), channel_id=1, source_target_pairs={{0,2},{1,3},{2,0},{3,1},{4,6},{5,7},{6,4},{7,5},{8,10},{9,11},{10,... | collective-permute-start | bytes 1966088 | tf_op jit(solution)/shard_map/ppermute | solution.py:606
  130.0 13.6 %collective-permute-start.24 = (f32[8,128]{1,0:T(8,128)S(1)}, f32[8,128]{1,0:T(8,128)S(1)}, u32[]{:S(2)}, u32[]{:S(2)}) collective-permute-start(f32[8,128]{1,0:T(8,128)S(1)} %broadcast_in_dim.42), channel_id=1, source_target_pairs={{0,1},{1,0},{2,3},{3,2},{4,5},{5,4},{6,7},{7,6},{8,9},{9,8},{10,11... | collective-permute-start | bytes 12296 | tf_op jit(solution)/shard_map/ppermute | solution.py:606
  140.4 8.7 %collective-permute-start.20 = (bf16[4,144,256]{2,1,0:T(8,128)(2,1)S(1)}, bf16[4,144,256]{2,1,0:T(8,128)(2,1)S(1)}, u32[]{:S(2)}, u32[]{:S(2)}) collective-permute-start(bf16[4,144,256]{2,1,0:T(8,128)(2,1)S(1)} %add_convert_fusion.3), channel_id=1, source_target_pairs={{0,2},{1,3},{2,0},{3,1},{4,6},{5,7},{6,4},{7,5},{8,10},{9,11},{10,... | collective-permute-start | bytes 884744 | tf_op jit(solution)/shard_map/ppermute | solution.py:606
  143.0 11.4 %copy-start.4 = (bf16[8,160,256]{2,1,0:T(8,128)(2,1)}, bf16[8,160,256]{2,1,0:T(8,128)(2,1)S(1)}, u32[]{:S(2)}) copy-start(bf16[8,160,256]{2,1,0:T(8,128)(2,1)S(1)} %collective-permute-done.13) | copy-start | bytes 1966084
  143.1 11.1 %collective-permute-start.14 = (bf16[4,160,256]{2,1,0:T(8,128)(2,1)S(1)}, bf16[4,160,256]{2,1,0:T(8,128)(2,1)S(1)}, u32[]{:S(2)}, u32[]{:S(2)}) collective-permute-start(bf16[4,160,256]{2,1,0:T(8,128)(2,1)S(1)} %add_convert_fusion.2), channel_id=1, source_target_pairs={{0,4},{1,5},{2,6},{3,7},{4,0},{5,1},{6,2},{7,3},{8,12},{9,13},{10,... | collective-permute-start | bytes 983048 | tf_op jit(solution)/shard_map/ppermute | solution.py:606
  143.7 23.8 %collective-permute-start.25 = (f32[8,128]{1,0:T(8,128)S(1)}, f32[8,128]{1,0:T(8,128)S(1)}, u32[]{:S(2)}, u32[]{:S(2)}) collective-permute-start(f32[8,128]{1,0:T(8,128)S(1)} %broadcast_add_fusion.1), channel_id=1, source_target_pairs={{0,2},{1,3},{2,0},{3,1},{4,6},{5,7},{6,4},{7,5},{8,10},{9,11},{10,... | collective-permute-start | bytes 12296 | tf_op jit(solution)/shard_map/ppermute | solution.py:606
  150.3 6.4 %collective-permute-start.21 = (bf16[1,144,256]{2,1,0:T(8,128)(2,1)S(1)}, bf16[1,144,256]{2,1,0:T(8,128)(2,1)S(1)}, u32[]{:S(2)}, u32[]{:S(2)}) collective-permute-start(bf16[1,144,256]{2,1,0:T(8,128)(2,1)S(1)} %get-tuple-element.40), channel_id=1, source_target_pairs={{0,8},{1,9},{2,10},{3,11},{4,12},{5,13},{6,14},{7,15},{8,16},{9,17... | collective-permute-start | bytes 221192 | tf_op jit(solution)/shard_map/ppermute | solution.py:606
  150.4 9.0 %collective-permute-start.22 = (bf16[1,144,256]{2,1,0:T(8,128)(2,1)S(1)}, bf16[1,144,256]{2,1,0:T(8,128)(2,1)S(1)}, u32[]{:S(2)}, u32[]{:S(2)}) collective-permute-start(bf16[1,144,256]{2,1,0:T(8,128)(2,1)S(1)} %get-tuple-element.42), channel_id=1, source_target_pairs={{0,16},{1,17},{2,18},{3,19},{4,20},{5,21},{6,22},{7,23},{8,24},{9,... | collective-permute-start | bytes 221192 | tf_op jit(solution)/shard_map/ppermute | solution.py:606
  150.9 11.1 %collective-permute-start.23 = (bf16[1,144,256]{2,1,0:T(8,128)(2,1)S(1)}, bf16[1,144,256]{2,1,0:T(8,128)(2,1)S(1)}, u32[]{:S(2)}, u32[]{:S(2)}) collective-permute-start(bf16[1,144,256]{2,1,0:T(8,128)(2,1)S(1)} %get-tuple-element.41), channel_id=1, source_target_pairs={{0,24},{1,25},{2,26},{3,27},{4,28},{5,29},{6,30},{7,31},{8,0},{9,1... | collective-permute-start | bytes 221192 | tf_op jit(solution)/shard_map/ppermute | solution.py:606
  154.4 8.7 %collective-permute-start.15 = (bf16[1,160,256]{2,1,0:T(8,128)(2,1)S(1)}, bf16[1,160,256]{2,1,0:T(8,128)(2,1)S(1)}, u32[]{:S(2)}, u32[]{:S(2)}) collective-permute-start(bf16[1,160,256]{2,1,0:T(8,128)(2,1)S(1)} %get-tuple-element.37), channel_id=1, source_target_pairs={{0,8},{1,9},{2,10},{3,11},{4,12},{5,13},{6,14},{7,15},{8,16},{9,17... | collective-permute-start | bytes 245768 | tf_op jit(solution)/shard_map/ppermute | solution.py:606
  156.8 8.3 %collective-permute-start.16 = (bf16[1,160,256]{2,1,0:T(8,128)(2,1)S(1)}, bf16[1,160,256]{2,1,0:T(8,128)(2,1)S(1)}, u32[]{:S(2)}, u32[]{:S(2)}) collective-permute-start(bf16[1,160,256]{2,1,0:T(8,128)(2,1)S(1)} %get-tuple-element.39), channel_id=1, source_target_pairs={{0,16},{1,17},{2,18},{3,19},{4,20},{5,21},{6,22},{7,23},{8,24},{9,... | collective-permute-start | bytes 245768 | tf_op jit(solution)/shard_map/ppermute | solution.py:606
  159.4 5.6 %collective-permute-start.17 = (bf16[1,160,256]{2,1,0:T(8,128)(2,1)S(1)}, bf16[1,160,256]{2,1,0:T(8,128)(2,1)S(1)}, u32[]{:S(2)}, u32[]{:S(2)}) collective-permute-start(bf16[1,160,256]{2,1,0:T(8,128)(2,1)S(1)} %get-tuple-element.38), channel_id=1, source_target_pairs={{0,24},{1,25},{2,26},{3,27},{4,28},{5,29},{6,30},{7,31},{8,0},{9,1... | collective-permute-start | bytes 245768 | tf_op jit(solution)/shard_map/ppermute | solution.py:606
  163.0 25.7 %copy-start.1 = (f32[77312]{0:T(1024)S(1)}, f32[77312]{0:T(1024)}, u32[]{:S(2)}) copy-start(f32[77312]{0:T(1024)} %param.8) | copy-start | bytes 927748
  163.0 25.7 %copy-start.5 = (f32[77312]{0:T(1024)S(1)}, f32[77312]{0:T(1024)}, u32[]{:S(2)}) copy-start(f32[77312]{0:T(1024)} %param.9) | copy-start | bytes 927748
  167.3 1.2 collective-permute-start.30
  167.5 3.7 %collective-permute-start.26 = (f32[8,128]{1,0:T(8,128)S(1)}, f32[8,128]{1,0:T(8,128)S(1)}, u32[]{:S(2)}, u32[]{:S(2)}) collective-permute-start(f32[8,128]{1,0:T(8,128)S(1)} %fusion.65), channel_id=1, source_target_pairs={{0,4},{1,5},{2,6},{3,7},{4,0},{5,1},{6,2},{7,3},{8,12},{9,13},{10,... | collective-permute-start | bytes 12296 | tf_op jit(solution)/shard_map/ppermute | solution.py:606
  169.2 6.2 %collective-permute-start.31 = (f32[8,128]{1,0:T(8,128)S(1)}, f32[8,128]{1,0:T(8,128)S(1)}, u32[]{:S(2)}, u32[]{:S(2)}) collective-permute-start(f32[8,128]{1,0:T(8,128)S(1)} %broadcast_add_fusion), channel_id=1, source_target_pairs={{0,2},{1,3},{2,0},{3,1},{4,6},{5,7},{6,4},{7,5},{8,10},{9,11},{10,... | collective-permute-start | bytes 12296 | tf_op jit(solution)/shard_map/ppermute | solution.py:606
  171.1 5.9 %collective-permute-start.27 = (f32[8,128]{1,0:T(8,128)S(1)}, f32[8,128]{1,0:T(8,128)S(1)}, u32[]{:S(2)}, u32[]{:S(2)}) collective-permute-start(f32[8,128]{1,0:T(8,128)S(1)} %add.1037), channel_id=1, source_target_pairs={{0,16},{1,17},{2,18},{3,19},{4,20},{5,21},{6,22},{7,23},{8,24},{9,... | collective-permute-start | bytes 12296 | tf_op jit(solution)/shard_map/ppermute | solution.py:606
  171.6 5.4 %collective-permute-start.28 = (f32[8,128]{1,0:T(8,128)S(1)}, f32[8,128]{1,0:T(8,128)S(1)}, u32[]{:S(2)}, u32[]{:S(2)}) collective-permute-start(f32[8,128]{1,0:T(8,128)S(1)} %add.1037), channel_id=1, source_target_pairs={{0,8},{1,9},{2,10},{3,11},{4,12},{5,13},{6,14},{7,15},{8,16},{9,17... | collective-permute-start | bytes 12296 | tf_op jit(solution)/shard_map/ppermute | solution.py:606
  174.9 3.6 %collective-permute-start.29 = (f32[8,128]{1,0:T(8,128)S(1)}, f32[8,128]{1,0:T(8,128)S(1)}, u32[]{:S(2)}, u32[]{:S(2)}) collective-permute-start(f32[8,128]{1,0:T(8,128)S(1)} %add.1037), channel_id=1, source_target_pairs={{0,24},{1,25},{2,26},{3,27},{4,28},{5,29},{6,30},{7,31},{8,0},{9,1... | collective-permute-start | bytes 12296 | tf_op jit(solution)/shard_map/ppermute | solution.py:606
  176.1 3.7 %collective-permute-start.32 = (f32[8,128]{1,0:T(8,128)S(1)}, f32[8,128]{1,0:T(8,128)S(1)}, u32[]{:S(2)}, u32[]{:S(2)}) collective-permute-start(f32[8,128]{1,0:T(8,128)S(1)} %fusion.66), channel_id=1, source_target_pairs={{0,4},{1,5},{2,6},{3,7},{4,0},{5,1},{6,2},{7,3},{8,12},{9,13},{10,... | collective-permute-start | bytes 12296 | tf_op jit(solution)/shard_map/ppermute | solution.py:606
  179.8 5.3 %collective-permute-start.33 = (f32[8,128]{1,0:T(8,128)S(1)}, f32[8,128]{1,0:T(8,128)S(1)}, u32[]{:S(2)}, u32[]{:S(2)}) collective-permute-start(f32[8,128]{1,0:T(8,128)S(1)} %add.1043), channel_id=1, source_target_pairs={{0,16},{1,17},{2,18},{3,19},{4,20},{5,21},{6,22},{7,23},{8,24},{9,... | collective-permute-start | bytes 12296 | tf_op jit(solution)/shard_map/ppermute | solution.py:606
  180.7 5.4 %collective-permute-start.34 = (f32[8,128]{1,0:T(8,128)S(1)}, f32[8,128]{1,0:T(8,128)S(1)}, u32[]{:S(2)}, u32[]{:S(2)}) collective-permute-start(f32[8,128]{1,0:T(8,128)S(1)} %add.1043), channel_id=1, source_target_pairs={{0,8},{1,9},{2,10},{3,11},{4,12},{5,13},{6,14},{7,15},{8,16},{9,17... | collective-permute-start | bytes 12296 | tf_op jit(solution)/shard_map/ppermute | solution.py:606
  181.9 4.1 %collective-permute-start.35 = (f32[8,128]{1,0:T(8,128)S(1)}, f32[8,128]{1,0:T(8,128)S(1)}, u32[]{:S(2)}, u32[]{:S(2)}) collective-permute-start(f32[8,128]{1,0:T(8,128)S(1)} %add.1043), channel_id=1, source_target_pairs={{0,24},{1,25},{2,26},{3,27},{4,28},{5,29},{6,30},{7,31},{8,0},{9,1... | collective-permute-start | bytes 12296 | tf_op jit(solution)/shard_map/ppermute | solution.py:606
  188.8 2.0 %copy-start.6 = (f32[77312]{0:T(1024)S(1)}, f32[77312]{0:T(1024)}, u32[]{:S(2)}) copy-start(f32[77312]{0:T(1024)} %param.11) | copy-start | bytes 927748
  (1 other events, 0.8 us)

commit v2 on v1

--- a/solution.py
+++ b/solution.py
@@ -23,82 +23,42 @@
 BF16 = jnp.bfloat16
 
 
-def block_entries(entries, prefix, width_in, with_res):
-    entries.append((prefix + "_conv1", K * width_in))
-    entries.append((prefix + "_bias1", 1))
-    entries.append((prefix + "_gain1", 1))
-    entries.append((prefix + "_shift1", 1))
-    entries.append((prefix + "_time", D))
-    entries.append((prefix + "_time_bias", 1))
-    entries.append((prefix + "_conv2", K * D))
-    entries.append((prefix + "_bias2", 1))
-    entries.append((prefix + "_gain2", 1))
-    entries.append((prefix + "_shift2", 1))
-    if with_res:
-        entries.append((prefix + "_res", width_in))
-        entries.append((prefix + "_res_bias", 1))
+TIME_FIRST, TIME_FIRST_BIAS, TIME_SECOND, TIME_SECOND_BIAS, INPUT_CONV, INPUT_BIAS = range(6)
+DOWN = 6
+DOWN_SAMPLE, DOWN_SAMPLE_BIAS, UP_SAMPLE, UP_SAMPLE_BIAS = range(16, 20)
+UP = 20
+UP_RES, UP_RES_BIAS, HEAD_MAT, HEAD_BIAS = range(30, 34)
+CONV1, BIAS1, GAIN1, SHIFT1, TIME, TIME_BIAS, CONV2, BIAS2, GAIN2, SHIFT2 = range(10)
 
 
 def layout():
-    entries = [
-        ("time_first", TE),
-        ("time_first_bias", 1),
-        ("time_second", D),
-        ("time_second_bias", 1),
-        ("input_conv", K * CH),
-        ("input_bias", 1),
-    ]
-    block_entries(entries, "down", D, False)
-    entries += [
-        ("down_sample", 3 * D),
-        ("down_sample_bias", 1),
-        ("up_sample", 4 * D),
-        ("up_sample_bias", 1),
-    ]
-    block_entries(entries, "up", 2 * D, True)
-    entries += [("head", CH), ("head_bias", 1)]
-    rows = {}
-    offset = 0
-    for label, count in entries:
-        rows[label] = (offset, count)
-        offset += count
-    return rows
+    counts = [TE, 1, D, 1, K * CH, 1]
+    counts += [K * D, 1, 1, 1, D, 1, K * D, 1, 1, 1]
+    counts += [3 * D, 1, 4 * D, 1]
+    counts += [2 * K * D, 1, 1, 1, D, 1, K * D, 1, 1, 1, 2 * D, 1]
+    counts += [CH, 1]
+    return [(sum(counts[:i]), count) for i, count in enumerate(counts)]
 
 
 ROWS = layout()
 MATS = (
-    "time_first",
-    "time_second",
-    "input_conv",
-    "down_conv1",
-    "down_time",
-    "down_conv2",
-    "down_sample",
-    "up_sample",
-    "up_conv1",
-    "up_time",
-    "up_conv2",
-    "up_res",
+    TIME_FIRST,
+    TIME_SECOND,
+    INPUT_CONV,
+    DOWN + CONV1,
+    DOWN + TIME,
+    DOWN + CONV2,
+    DOWN_SAMPLE,
+    UP_SAMPLE,
+    UP + CONV1,
+    UP + TIME,
+    UP + CONV2,
+    UP_RES,
 )
-SUMS = (
-    "input_bias",
-    "down_bias1",
-    "down_gain1",
-    "down_shift1",
-    "down_bias2",
-    "down_gain2",
-    "down_shift2",
-    "down_sample_bias",
-    "up_sample_bias",
-    "up_bias1",
-    "up_gain1",
-    "up_shift1",
-    "up_bias2",
-    "up_gain2",
-    "up_shift2",
-    "up_res_bias",
+SUMS = (INPUT_BIAS, DOWN_SAMPLE_BIAS, UP_SAMPLE_BIAS, UP_RES_BIAS) + tuple(
+    block + piece for block in (DOWN, UP) for piece in (BIAS1, GAIN1, SHIFT1, BIAS2, GAIN2, SHIFT2)
 )
-NORMS = ("down1", "down2", "up1", "up2")
+NORMS = 4
 
 
 def up_to(value, step):
@@ -231,7 +191,7 @@
         for j in range(2):
             t_u1[K * D : K * D + D, j * D : j * D + D] = w_res[j * D : j * D + D, :].T
 
-        first = ROWS["head"][0]
+        first = ROWS[HEAD_MAT][0]
         head_rows = flat[first : first + 8, :].astype(BF16)
         at_row = lax.broadcasted_iota(jnp.int32, (D, D), 0)
         at_col = lax.broadcasted_iota(jnp.int32, (D, D), 1)
@@ -249,18 +209,18 @@
             spread = mm(head_rows, picker(j))
             headT[j : j + 1, :] = jnp.sum(jnp.where(picked(j), spread, 0.0), axis=0, keepdims=True)
         head_b = headT[...].astype(BF16)
-        head_bias = row("head_bias")[:, :HEAD]
+        head_bias = row(HEAD_BIAS)[:, :HEAD]
         head_bias = jnp.where(lax.broadcasted_iota(jnp.int32, (1, HEAD), 1) < CH, head_bias, 0.0)
 
         emb_b = emb[...]
-        z1 = mm(emb_b, w_tf[...]) + row("time_first_bias")
+        z1 = mm(emb_b, w_tf[...]) + row(TIME_FIRST_BIAS)
         t1, slope1 = mish_pair(z1)
         t1 = t1.astype(BF16)
-        z2 = mm(t1, w_ts[...]) + row("time_second_bias")
+        z2 = mm(t1, w_ts[...]) + row(TIME_SECOND_BIAS)
         t2, slope2 = mish_pair(z2)
         timing = t2.astype(BF16)
-        temb_d[...] = mm(timing, w_dt[...]) + row("down_time_bias")
-        temb_u[...] = mm(timing, w_ut[...]) + row("up_time_bias")
+        temb_d[...] = mm(timing, w_dt[...]) + row(DOWN + TIME_BIAS)
+        temb_u[...] = mm(timing, w_ut[...]) + row(UP + TIME_BIAS)
 
         def add_sum(label, value):
             i = SUMS.index(label)
@@ -292,8 +252,8 @@
                 mp[which, c, :] = slope
                 write(c, value)
 
-        def norm_backward(which, index, h, prefix, number):
-            gain = row(prefix + "_gain" + number)
+        def norm_backward(which, index, h, block, second):
+            gain = row(block + GAIN1 + second)
             one = zero8
             two = zero8
             for c in chunks:
@@ -301,8 +261,8 @@
                 one = one + fold(dv)
                 two = two + fold(dv * xhat[which, c, :])
                 dbuf[c, :] = dv
-            add_sum(prefix + "_shift" + number, one)
-            add_sum(prefix + "_gain" + number, two)
+            add_sum(block + SHIFT1 + second, one)
+            add_sum(block + GAIN1 + second, two)
             mean1, mean2 = group_sums([one * gain, two * gain], ones[...])
             rstd = rstds[index, pl.ds(h, 1), :]
             scale = rstd * gain
@@ -313,7 +273,7 @@
                 dc = dbuf[c, :] * scale - mean1 - xhat[which, c, :] * mean2
                 pad_set(padA, c.start + 8, dc)
                 total = total + fold(dc)
-            add_sum(prefix + "_bias" + number, total)
+            add_sum(block + BIAS1 + second, total)
 
         def rounded_to_dbuf(value):
             dbuf[...] = value.astype(BF16).astype(F32)
@@ -330,13 +290,13 @@
             base2 = pl.multiple_of(h * half, CHUNK)
             rows = pl.ds(base, length)
             rows2 = pl.ds(base2, half)
-            entry[...] = mm(xin[h], w_in[...]) + row("input_bias")
+            entry[...] = mm(xin[h], w_in[...]) + row(INPUT_BIAS)
             for c in chunks:
                 value = entry[c, :]
                 pad_set(padA, c.start + 8, value)
                 x_d1[pl.ds(base + c.start, CHUNK), :] = value.astype(BF16)
             shifted(cols, 0, D, K * D, 1)
-            cbuf[...] = mm(cols[:, : K * D], w_d1[...]) + row("down_bias1")
+            cbuf[...] = mm(cols[:, : K * D], w_d1[...]) + row(DOWN + BIAS1)
             time_row = temb_d[pl.ds(h, 1), :]
 
             def write_d1(c, value):
@@ -344,26 +304,26 @@
                 pad_set(padA, c.start + 8, value)
                 x_d2[pl.ds(base + c.start, CHUNK), :] = value.astype(BF16)
 
-            norm_forward(2 + 2 * h, 0, h, row("down_gain1"), row("down_shift1"), write_d1)
+            norm_forward(2 + 2 * h, 0, h, row(DOWN + GAIN1), row(DOWN + SHIFT1), write_d1)
             shifted(cols, 0, D, K * D, 1)
-            cbuf[...] = mm(cols[:, : K * D], w_d2[...]) + row("down_bias2")
+            cbuf[...] = mm(cols[:, : K * D], w_d2[...]) + row(DOWN + BIAS2)
 
             def write_d2(c, value):
                 pad_set(padS, c.start + 8, value + entry[c, :])
 
-            norm_forward(3 + 2 * h, 1, h, row("down_gain2"), row("down_shift2"), write_d2)
+            norm_forward(3 + 2 * h, 1, h, row(DOWN + GAIN2), row(DOWN + SHIFT2), write_d2)
             odd_before = pad_get(padS, 7, half, 2).astype(BF16)
             even = pad_get(padS, 8, half, 2).astype(BF16)
             odd = pad_get(padS, 9, half, 2).astype(BF16)
             x_e[rows2, :] = even
             x_o[rows2, :] = odd
-            coarse = mm(jnp.concatenate([odd_before, even, odd], axis=1), w_ds[...]) + row("down_sample_bias")
+            coarse = mm(jnp.concatenate([odd_before, even, odd], axis=1), w_ds[...]) + row(DOWN_SAMPLE_BIAS)
             pad_set(padY, 8, coarse)
             now = coarse.astype(BF16)
             x_y[rows2, :] = now
             before = pad_get(padY, 7, half).astype(BF16)
             after = pad_get(padY, 9, half).astype(BF16)
-            up_bias = row("up_sample_bias")
+            up_bias = row(UP_SAMPLE_BIAS)
             pad_set(padR, 8, mm(now, w_us[D : 2 * D, :]) + mm(before, w_us[3 * D : 4 * D, :]) + up_bias, 2)
             pad_set(padR, 9, mm(after, w_us[0:D, :]) + mm(now, w_us[2 * D : 3 * D, :]) + up_bias, 2)
             for k in range(K):
@@ -373,8 +333,8 @@
                     cols[c, 2 * k * D + D : 2 * k * D + 2 * D] = pad_get(padS, start + c.start, CHUNK).astype(BF16)
             middle = 2 * (K // 2) * D
             x_j[rows, :] = cols[:, middle : middle + 2 * D]
-            rbuf[...] = mm(cols[:, middle : middle + 2 * D], w_res[...]) + row("up_res_bias")
-            cbuf[...] = mm(cols[...], w_u1[...]) + row("up_bias1")
+            rbuf[...] = mm(cols[:, middle : middle + 2 * D], w_res[...]) + row(UP_RES_BIAS)
+            cbuf[...] = mm(cols[...], w_u1[...]) + row(UP + BIAS1)
             time_up = temb_u[pl.ds(h, 1), :]
 
             def write_u1(c, value):
@@ -382,14 +342,14 @@
                 pad_set(padA, c.start + 8, value)
                 x_u2[pl.ds(base + c.start, CHUNK), :] = value.astype(BF16)
 
-            norm_forward(0, 2, h, row("up_gain1"), row("up_shift1"), write_u1)
+            norm_forward(0, 2, h, row(UP + GAIN1), row(UP + SHIFT1), write_u1)
             shifted(cols, 0, D, K * D, 1)
-            cbuf[...] = mm(cols[:, : K * D], w_u2[...]) + row("up_bias2")
+            cbuf[...] = mm(cols[:, : K * D], w_u2[...]) + row(UP + BIAS2)
 
             def write_u2(c, value):
                 topb[c, :] = (value + rbuf[c, :]).astype(BF16)
 
-            norm_forward(1, 3, h, row("up_gain2"), row("up_shift2"), write_u2)
+            norm_forward(1, 3, h, row(UP + GAIN2), row(UP + SHIFT2), write_u2)
             prediction = mm_nt(topb[...], head_b) + head_bias
             frame = lax.broadcasted_iota(jnp.int32, (length, HEAD), 0)
             error = jnp.where(frame < lens[h], prediction - noise[h], 0.0)
@@ -401,19 +361,19 @@
             dtop = mm(error, head_b).astype(BF16)
             dy1[rows, K * D : (K + 1) * D] = dtop
             dbuf[...] = dtop.astype(F32)
-            add_sum("up_res_bias", column_sum())
-            norm_backward(1, 3, h, "up", "2")
+            add_sum(UP_RES_BIAS, column_sum())
+            norm_backward(1, 3, h, UP, CONV2)
             shifted(dy2, base, D, K * D, -1)
             rounded_to_dbuf(mm(dy2[rows, :], t_u2[...]))
             dtemb_u[pl.ds(h, 1), :] = jnp.sum(column_sum(), axis=0, keepdims=True)
-            norm_backward(0, 2, h, "up", "1")
+            norm_backward(0, 2, h, UP, 0)
             shifted(dy1, base, D, K * D, -1)
             dbuf[...] = mm(dy1[rows, :], t_u1[:, D:]).astype(BF16).astype(F32)
             pad_set(padR, 8, mm(dy1[rows, :], t_u1[:, :D]).astype(BF16).astype(F32))
             total = zero8
             for c in chunks:
                 total = total + fold(pad_get(padR, c.start + 8, CHUNK))
-            add_sum("up_sample_bias", total)
+            add_sum(UP_SAMPLE_BIAS, total)
             dy4[rows2, 0:D] = pad_get(padR, 7, half, 2).astype(BF16)
             dy4[rows2, D : 2 * D] = pad_get(padR, 8, half, 2).astype(BF16)
             dy4[rows2, 2 * D : 3 * D] = pad_get(padR, 9, half, 2).astype(BF16)
@@ -421,7 +381,7 @@
             dcoarse = mm(dy4[rows2, :], t_us[...]).astype(BF16)
             dcoarse32 = dcoarse.astype(F32)
             pad_set(padY, 8, dcoarse32)
-            add_sum("down_sample_bias", fold(dcoarse32))
+            add_sum(DOWN_SAMPLE_BIAS, fold(dcoarse32))
             dyc[rows2, 0:D] = pad_get(padY, 9, half).astype(BF16)
             dyc[rows2, D : 2 * D] = dcoarse
             dodd = mm(dyc[rows2, :], t_ds[0 : 2 * D, :]).astype(BF16).astype(F32)
@@ -442,23 +402,23 @@
                 put(label, offset, mm(xt[0:width, 0:rows], dy[:, block * D : block * D + D]))
 
         weight_grads(
-            x_j, 2 * D, rows_all, dy1, [("up_conv1", 2 * k * D, k) for k in range(K)] + [("up_res", 0, K)]
+            x_j, 2 * D, rows_all, dy1, [(UP + CONV1, 2 * k * D, k) for k in range(K)] + [(UP_RES, 0, K)]
         )
-        weight_grads(x_u2, D, rows_all, dy2, [("up_conv2", k * D, k) for k in range(K)])
-        weight_grads(x_y, D, halves_all, dy4, [("up_sample", k * D, k) for k in range(4)])
-        weight_grads(x_o, D, halves_all, dyc, [("down_sample", 0, 0), ("down_sample", 2 * D, 1)])
-        weight_grads(x_e, D, halves_all, dyc, [("down_sample", D, 1)])
+        weight_grads(x_u2, D, rows_all, dy2, [(UP + CONV2, k * D, k) for k in range(K)])
+        weight_grads(x_y, D, halves_all, dy4, [(UP_SAMPLE, k * D, k) for k in range(4)])
+        weight_grads(x_o, D, halves_all, dyc, [(DOWN_SAMPLE, 0, 0), (DOWN_SAMPLE, 2 * D, 1)])
+        weight_grads(x_e, D, halves_all, dyc, [(DOWN_SAMPLE, D, 1)])
 
         @pl.loop(0, horizons)
         def _(h):
             base = pl.multiple_of(h * length, CHUNK)
             rows = pl.ds(base, length)
             dbuf[...] = dskip[h]
-            norm_backward(3 + 2 * h, 1, h, "down", "2")
+            norm_backward(3 + 2 * h, 1, h, DOWN, CONV2)
             shifted(dy2, base, D, K * D, -1)
             rounded_to_dbuf(mm(dy2[rows, :], t_d2[...]))
             dtemb_d[pl.ds(h, 1), :] = jnp.sum(column_sum(), axis=0, keepdims=True)
-            norm_backward(2 + 2 * h, 0, h, "down", "1")
+            norm_backward(2 + 2 * h, 0, h, DOWN, 0)
             shifted(dy1, base, D, K * D, -1)
             rounded_to_dbuf(mm(dy1[rows, : K * D], t_d1[...]))
             total = zero8
@@ -466,44 +426,44 @@
                 value = dbuf[c, :] + dskip[h, c, :]
                 total = total + fold(value)
                 dent[pl.ds(base + c.start, CHUNK), :] = value.astype(BF16)
-            add_sum("input_bias", total)
-
-        weight_grads(x_d2, D, rows_all, dy2, [("down_conv2", k * D, k) for k in range(K)])
-        weight_grads(x_d1, D, rows_all, dy1, [("down_conv1", k * D, k) for k in range(K)])
+            add_sum(INPUT_BIAS, total)
+
+        weight_grads(x_d2, D, rows_all, dy2, [(DOWN + CONV2, k * D, k) for k in range(K)])
+        weight_grads(x_d1, D, rows_all, dy1, [(DOWN + CONV1, k * D, k) for k in range(K)])
         inputs = zero8
         for h in range(horizons):
             part = mm_tn(xin[h], dent[h * length : h * length + length, :])
             inputs = part if h == 0 else inputs + part
-        put("input_conv", 0, inputs[: K * CH])
+        put(INPUT_CONV, 0, inputs[: K * CH])
 
         down_b = dtemb_d[...].astype(BF16)
         up_b = dtemb_u[...].astype(BF16)
-        put("down_time", 0, mm_tn(timing, down_b))
-        put("up_time", 0, mm_tn(timing, up_b))
+        put(DOWN + TIME, 0, mm_tn(timing, down_b))
+        put(UP + TIME, 0, mm_tn(timing, up_b))
         dtiming = (mm_nt(down_b, w_dt[...]) + mm_nt(up_b, w_ut[...])).astype(BF16).astype(F32)
         dz2 = dtiming * slope2
         dz2_b = dz2.astype(BF16)
-        put("time_second", 0, mm_tn(t1, dz2_b))
+        put(TIME_SECOND, 0, mm_tn(t1, dz2_b))
         dz1 = mm_nt(dz2_b, w_ts[...]).astype(BF16).astype(F32) * slope1
-        put("time_first", 0, mm_tn(emb_b, dz1.astype(BF16)))
+        put(TIME_FIRST, 0, mm_tn(emb_b, dz1.astype(BF16)))
         for label, value in (
-            ("time_first_bias", dz1),
-            ("time_second_bias", dz2),
-            ("down_time_bias", dtemb_d[...]),
-            ("up_time_bias", dtemb_u[...]),
+            (TIME_FIRST_BIAS, dz1),
+            (TIME_SECOND_BIAS, dz2),
+            (DOWN + TIME_BIAS, dtemb_d[...]),
+            (UP + TIME_BIAS, dtemb_u[...]),
         ):
             put(label, 0, jnp.sum(value, axis=0, keepdims=True))
         for i, label in enumerate(SUMS):
             put(label, 0, jnp.sum(sums[i], axis=0, keepdims=True))
 
-        tail = ROWS["head"][0]
+        tail = ROWS[HEAD_MAT][0]
         flat[tail : total_rows + 16, :] = jnp.zeros((total_rows + 16 - tail, D), F32)
         packed = jnp.zeros((8, D), F32)
         for j in range(CH):
             spread = jnp.where(picked(j), jnp.broadcast_to(dheadT[j : j + 1, :], (8, D)), 0.0)
             packed = packed + mm_nt(spread.astype(BF16), picker(j))
-        put("head", 0, packed[:CH])
-        first = ROWS["head_bias"][0]
+        put(HEAD_MAT, 0, packed[:CH])
+        first = ROWS[HEAD_BIAS][0]
         flat[first : first + 1, 0:HEAD] = jnp.sum(hsum[...], axis=0, keepdims=True)
 
         for s in range(n):
@@ -545,7 +505,7 @@
         vm((2 + 2 * horizons, length, D), F32),
         vm((2 + 2 * horizons, length, D), F32),
         vm((horizons, length, D), F32),
-        vm((len(NORMS), 8, D), F32),
+        vm((NORMS, 8, D), F32),
         vm((16, D), F32),
         vm((16, D), F32),
         vm((16, D), F32),
@@ -580,7 +540,7 @@
         scratch_shapes=scratch,
         compiler_params=pltpu.CompilerParams(vmem_limit_bytes=63 * 1024 * 1024),
         cost_estimate=pl.CostEstimate(flops=flops, bytes_accessed=10000000, transcendentals=3000000),
-        name="train_step",
+        name="step",
     )
 
 

time: 193 us -> 193 us (level)
  transfers between devices with their start and end apart: 36 -> 36, of which waited for: 15 -> 16; matrix products, arithmetic and copies ran while one was open for 15% -> 15% of each run, Pallas kernels for 0% -> 0%
where the time goes in v2:
time: 193 us
  Pallas kernels  62.5 us (32%)
  waiting for transfers between devices  47.7 us (25%)
  starting transfers between devices  43.5 us (23%)
  other arithmetic  18.3 us (9%)
  local copies, waits for them, and re-layouts  16.6 us (9%)
  between operations  4.28 us (2%)
    pallas_call x1, Pallas kernels, shards(): call(ring.table(me, order_a), ring.table(me, order_b), lens, xin, noise8,...  62.5 us
    ppermute x36, waiting for transfers between devices, send(): lax.ppermute(values, 'batch', [(i, self.moved(i, axis, step)) for i in ra...  47.7 us
    ppermute x36, starting transfers between devices, send(): lax.ppermute(values, 'batch', [(i, self.moved(i, axis, step)) for i in ra...  43.5 us
    convert_element_type x6, other arithmetic, scatter(): part = sum((term[step].astype(F32) for term in cut)).astype(BF16)  6.22 us
    unnamed x36, local copies, waits for them, and re-layouts  5.77 us
  transfers between devices with their start and end apart: 36, of which 16 were waited for; matrix products, arithmetic and copies ran while one was open for 15% of the time, Pallas kernels for 0%

profile of v2, /device:TPU:0, one launch (start us, length us, event | category | flops | bytes accessed | tf_op | source)
XLA Modules:
  0.0 192.8 jit_solution(748308429631243995)
XLA Ops:
  0.6 1.0 convert_element_type.309
  1.7 5.1 %collective-permute-start.6 = (bf16[1,144,256]{2,1,0:T(8,128)(2,1)S(1)}, bf16[1,144,256]{2,1,0:T(8,128)(2,1)S(1)}, u32[]{:S(2)}, u32[]{:S(2)}) collective-permute-start(bf16[1,144,256]{2,1,0:T(8,128)(2,1)S(1)} %fusion.4), channel_id=1, source_target_pairs={{0,24},{1,25},{2,26},{3,27},{4,28},{5,29},{6,30},{7,31},{8,0},{9,1... | collective-permute-start | bytes 221192 | tf_op jit(solution)/shard_map/ppermute | solution.py:566
  6.8 1.0 collective-permute-start.8
  7.9 2.9 %collective-permute-start = (bf16[1,160,256]{2,1,0:T(8,128)(2,1)S(1)}, bf16[1,160,256]{2,1,0:T(8,128)(2,1)S(1)}, u32[]{:S(2)}, u32[]{:S(2)}) collective-permute-start(bf16[1,160,256]{2,1,0:T(8,128)(2,1)S(1)} %broadcast_in_dim.37), channel_id=1, source_target_pairs={{0,24},{1,25},{2,26},{3,27},{4,28},{5,29},{6,30},{7,31},{8,0},{9,1... | collective-permute-start | bytes 245768 | tf_op jit(solution)/shard_map/ppermute | solution.py:566
  10.7 1.1 collective-permute-start.1
  15.0 1.6 collective-permute-start.9
  18.4 2.5 %collective-permute-done.1 = bf16[1,160,256]{2,1,0:T(8,128)(2,1)S(1)} collective-permute-done((bf16[1,160,256]{2,1,0:T(8,128)(2,1)S(1)}, bf16[1,160,256]{2,1,0:T(8,128)(2,1)S(1)}, u32[]{:S(2)}, u32[]{:S(2)}) %collective-permute-start.1) | collective-permute-done | bytes 81952 | tf_op jit(solution)/shard_map/ppermute | solution.py:566
  20.9 1.6 collective-permute-start.3
  24.5 6.1 %collective-permute-done.3 = bf16[4,160,256]{2,1,0:T(8,128)(2,1)S(1)} collective-permute-done((bf16[4,160,256]{2,1,0:T(8,128)(2,1)S(1)}, bf16[4,160,256]{2,1,0:T(8,128)(2,1)S(1)}, u32[]{:S(2)}, u32[]{:S(2)}) %collective-permute-start.3) | collective-permute-done | bytes 327712 | tf_op jit(solution)/shard_map/ppermute | solution.py:566
  31.3 1.5 collective-permute-start.4
  33.6 1.5 collective-permute-start.10
  36.0 11.0 %collective-permute-done.4 = bf16[8,160,256]{2,1,0:T(8,128)(2,1)S(1)} collective-permute-done((bf16[8,160,256]{2,1,0:T(8,128)(2,1)S(1)}, bf16[8,160,256]{2,1,0:T(8,128)(2,1)S(1)}, u32[]{:S(2)}, u32[]{:S(2)}) %collective-permute-start.4) | collective-permute-done | bytes 655392 | tf_op jit(solution)/shard_map/ppermute | solution.py:566
  47.1 0.9 constant_dynamic-update-slice_fusion.5.a0
  48.0 0.9 constant_dynamic-update-slice_fusion.16.b0
  50.7 0.9 pad.17.noise
  52.6 2.0 %concatenate.32.xin = bf16[4,384,32]{2,1,0:T(8,128)(2,1)} concatenate(bf16[4,384,6]{2,1,0:T(8,128)(2,1)S(1)} %get-tuple-element.46, bf16[4,384,6]{2,1,0:T(8,128)(2,1)S(1)} %get-tuple-element.44, bf16[4,384,6]{2,1,0:T(8,128)(2,1)S(1)} %fusion.2, bf16[4,384,6]{2,1,0:T(8,128)(2,1)S(1)} %get-tuple-element.45, bf16[4,384,6]{2,1,0:T(8,128)(2,1)S(1)} %get-tuple-element.43, ...), dimensions={2} | concatenate | bytes 196608 | tf_op jit(solution)/shard_map/concatenate | solution.py:628
  55.4 62.5 %step.1 = (bf16[16,160,256]{2,1,0:T(8,128)(2,1)}, bf16[16,160,256]{2,1,0:T(8,128)(2,1)}, bf16[16,144,256]{2,1,0:T(8,128)(2,1)}, bf16[16,144,256]{2,1,0:T(8,128)(2,1)}, f32[8,8]{1,0:T(8,128)}) custom-call(s32[32]{0:T(128)} %reshape.1866.tab_a, s32[32]{0:T(128)} %reshape.1869.tab_b, s32[4]{0:T(128)} %copy-done.12, bf16[4,384,32]{2,1,0:T(8,128)(2,1)} %concatenate.32.xin, ...), custom_call_target="tpu_custom_call" | custom-call | flops 19353600000 | bytes 10000000 | tf_op jit(solution)/shard_map/step/pallas_call | solution.py:658
  118.4 2.5 %collective-permute-done.18 = bf16[16,144,256]{2,1,0:T(8,128)(2,1)S(1)} collective-permute-done((bf16[16,144,256]{2,1,0:T(8,128)(2,1)}, bf16[16,144,256]{2,1,0:T(8,128)(2,1)S(1)}, u32[]{:S(2)}, u32[]{:S(2)}) %collective-permute-start.18) | collective-permute-done | bytes 1179680 | tf_op jit(solution)/shard_map/ppermute | solution.py:566
  121.0 2.4 %add_convert_fusion.1 = bf16[8,144,256]{2,1,0:T(8,128)(2,1)} fusion(bf16[16,144,256]{2,1,0:T(8,128)(2,1)S(1)} %collective-permute-done.18, bf16[16,144,256]{2,1,0:T(8,128)(2,1)} %get-tuple-element.15), kind=kLoop, calls=%fused_computation.1 | loop fusion | flops 1179648 | bytes 1769472 | tf_op jit(solution)/shard_map/convert_element_type | solution.py:592
  123.4 1.5 collective-permute-start.19
  125.0 1.0 add_convert_fusion
  126.0 1.5 collective-permute-start.13
  130.1 9.0 %collective-permute-done.19 = bf16[8,144,256]{2,1,0:T(8,128)(2,1)} collective-permute-done((bf16[8,144,256]{2,1,0:T(8,128)(2,1)}, bf16[8,144,256]{2,1,0:T(8,128)(2,1)}, u32[]{:S(2)}, u32[]{:S(2)}) %collective-permute-start.19) | collective-permute-done | bytes 589856 | tf_op jit(solution)/shard_map/ppermute | solution.py:566
  139.1 1.2 add_convert_fusion.3
  140.4 1.6 collective-permute-start.20
  141.9 1.0 collective-permute-done.13
  143.7 1.2 collective-permute-start.25
  144.9 4.2 %collective-permute-done.20 = bf16[4,144,256]{2,1,0:T(8,128)(2,1)S(1)} collective-permute-done((bf16[4,144,256]{2,1,0:T(8,128)(2,1)S(1)}, bf16[4,144,256]{2,1,0:T(8,128)(2,1)S(1)}, u32[]{:S(2)}, u32[]{:S(2)}) %collective-permute-start.20) | collective-permute-done | bytes 294944 | tf_op jit(solution)/shard_map/ppermute | solution.py:566
  149.1 1.3 add_convert_fusion.9
  150.9 3.4 %collective-permute-start.23 = (bf16[1,144,256]{2,1,0:T(8,128)(2,1)S(1)}, bf16[1,144,256]{2,1,0:T(8,128)(2,1)S(1)}, u32[]{:S(2)}, u32[]{:S(2)}) collective-permute-start(bf16[1,144,256]{2,1,0:T(8,128)(2,1)S(1)} %get-tuple-element.41), channel_id=1, source_target_pairs={{0,24},{1,25},{2,26},{3,27},{4,28},{5,29},{6,30},{7,31},{8,0},{9,1... | collective-permute-start | bytes 221192 | tf_op jit(solution)/shard_map/ppermute | solution.py:566
  155.0 1.8 collective-permute-done.21
  156.8 2.7 %collective-permute-done.22 = bf16[1,144,256]{2,1,0:T(8,128)(2,1)S(1)} collective-permute-done((bf16[1,144,256]{2,1,0:T(8,128)(2,1)S(1)}, bf16[1,144,256]{2,1,0:T(8,128)(2,1)S(1)}, u32[]{:S(2)}, u32[]{:S(2)}) %collective-permute-start.22) | collective-permute-done | bytes 73760 | tf_op jit(solution)/shard_map/ppermute | solution.py:566
  159.5 2.5 %collective-permute-start.17 = (bf16[1,160,256]{2,1,0:T(8,128)(2,1)S(1)}, bf16[1,160,256]{2,1,0:T(8,128)(2,1)S(1)}, u32[]{:S(2)}, u32[]{:S(2)}) collective-permute-start(bf16[1,160,256]{2,1,0:T(8,128)(2,1)S(1)} %get-tuple-element.38), channel_id=1, source_target_pairs={{0,24},{1,25},{2,26},{3,27},{4,28},{5,29},{6,30},{7,31},{8,0},{9,1... | collective-permute-start | bytes 245768 | tf_op jit(solution)/shard_map/ppermute | solution.py:566
  162.0 1.0 add_bitcast_fusion.1
  163.1 2.0 %collective-permute-done.16 = bf16[1,160,256]{2,1,0:T(8,128)(2,1)S(1)} collective-permute-done((bf16[1,160,256]{2,1,0:T(8,128)(2,1)S(1)}, bf16[1,160,256]{2,1,0:T(8,128)(2,1)S(1)}, u32[]{:S(2)}, u32[]{:S(2)}) %collective-permute-start.16) | collective-permute-done | bytes 81952 | tf_op jit(solution)/shard_map/ppermute | solution.py:566
  165.1 1.0 add_bitcast_fusion
  167.5 1.1 collective-permute-start.26
  169.3 1.5 collective-permute-start.31
  171.7 3.2 %collective-permute-start.28 = (f32[8,128]{1,0:T(8,128)S(1)}, f32[8,128]{1,0:T(8,128)S(1)}, u32[]{:S(2)}, u32[]{:S(2)}) collective-permute-start(f32[8,128]{1,0:T(8,128)S(1)} %add.1037), channel_id=1, source_target_pairs={{0,8},{1,9},{2,10},{3,11},{4,12},{5,13},{6,14},{7,15},{8,16},{9,17... | collective-permute-start | bytes 12296 | tf_op jit(solution)/shard_map/ppermute | solution.py:566
  176.1 0.9 collective-permute-start.32
  177.1 1.4 collective-permute-done.29
  178.5 1.3 collective-permute-done.32
  179.8 0.9 collective-permute-start.33
  180.7 1.3 collective-permute-start.34
  182.0 2.5 %collective-permute-start.35 = (f32[8,128]{1,0:T(8,128)S(1)}, f32[8,128]{1,0:T(8,128)S(1)}, u32[]{:S(2)}, u32[]{:S(2)}) collective-permute-start(f32[8,128]{1,0:T(8,128)S(1)} %add.1043), channel_id=1, source_target_pairs={{0,24},{1,25},{2,26},{3,27},{4,28},{5,29},{6,30},{7,31},{8,0},{9,1... | collective-permute-start | bytes 12296 | tf_op jit(solution)/shard_map/ppermute | solution.py:566
  185.1 1.0 collective-permute-done.34
  188.8 2.0 %fusion.61 = (bf16[77312]{0:T(1024)(128)(2,1)}, f32[77312]{0:T(1024)S(1)}, f32[77312]{0:T(1024)}, f32[77312]{0:T(1024)}) fusion(f32[77312]{0:T(1024)S(1)} %copy-done.1, f32[77312]{0:T(1024)S(1)} %mul.306, f32[77312]{0:T(1024)S(1)} %copy-done.5, f32[77312]{0:T(1024)} %param.10), kind=kLoop, calls=%fused_computation.229 | loop fusion | flops 1236992 | bytes 2319360 | tf_op jit(solution)/shard_map/convert_element_type | solution.py:683
  190.8 0.8 multiply_add_fusion
  (142 shorter events, 23.6 us)
Async XLA Ops:
  0.6 13.4 %copy-start.10 = (s32[2,2]{1,0:T(2,128)S(1)}, s32[2,2]{1,0:T(2,128)}, u32[]{:S(2)}) copy-start(s32[2,2]{1,0:T(2,128)} %param.14) | copy-start | bytes 52
  1.7 12.5 %collective-permute-start.6 = (bf16[1,144,256]{2,1,0:T(8,128)(2,1)S(1)}, bf16[1,144,256]{2,1,0:T(8,128)(2,1)S(1)}, u32[]{:S(2)}, u32[]{:S(2)}) collective-permute-start(bf16[1,144,256]{2,1,0:T(8,128)(2,1)S(1)} %fusion.4), channel_id=1, source_target_pairs={{0,24},{1,25},{2,26},{3,27},{4,28},{5,29},{6,30},{7,31},{8,0},{9,1... | collective-permute-start | bytes 221192 | tf_op jit(solution)/shard_map/ppermute | solution.py:566
  6.8 8.1 %collective-permute-start.7 = (bf16[1,144,256]{2,1,0:T(8,128)(2,1)S(1)}, bf16[1,144,256]{2,1,0:T(8,128)(2,1)S(1)}, u32[]{:S(2)}, u32[]{:S(2)}) collective-permute-start(bf16[1,144,256]{2,1,0:T(8,128)(2,1)S(1)} %fusion.4), channel_id=1, source_target_pairs={{0,16},{1,17},{2,18},{3,19},{4,20},{5,21},{6,22},{7,23},{8,24},{9,... | collective-permute-start | bytes 221192 | tf_op jit(solution)/shard_map/ppermute | solution.py:566
  6.8 8.1 %collective-permute-start.8 = (bf16[1,144,256]{2,1,0:T(8,128)(2,1)S(1)}, bf16[1,144,256]{2,1,0:T(8,128)(2,1)S(1)}, u32[]{:S(2)}, u32[]{:S(2)}) collective-permute-start(bf16[1,144,256]{2,1,0:T(8,128)(2,1)S(1)} %fusion.4), channel_id=1, source_target_pairs={{0,8},{1,9},{2,10},{3,11},{4,12},{5,13},{6,14},{7,15},{8,16},{9,17... | collective-permute-start | bytes 221192 | tf_op jit(solution)/shard_map/ppermute | solution.py:566
  7.9 10.5 %collective-permute-start = (bf16[1,160,256]{2,1,0:T(8,128)(2,1)S(1)}, bf16[1,160,256]{2,1,0:T(8,128)(2,1)S(1)}, u32[]{:S(2)}, u32[]{:S(2)}) collective-permute-start(bf16[1,160,256]{2,1,0:T(8,128)(2,1)S(1)} %broadcast_in_dim.37), channel_id=1, source_target_pairs={{0,24},{1,25},{2,26},{3,27},{4,28},{5,29},{6,30},{7,31},{8,0},{9,1... | collective-permute-start | bytes 245768 | tf_op jit(solution)/shard_map/ppermute | solution.py:566
  10.7 10.1 %collective-permute-start.1 = (bf16[1,160,256]{2,1,0:T(8,128)(2,1)S(1)}, bf16[1,160,256]{2,1,0:T(8,128)(2,1)S(1)}, u32[]{:S(2)}, u32[]{:S(2)}) collective-permute-start(bf16[1,160,256]{2,1,0:T(8,128)(2,1)S(1)} %broadcast_in_dim.37), channel_id=1, source_target_pairs={{0,16},{1,17},{2,18},{3,19},{4,20},{5,21},{6,22},{7,23},{8,24},{9,... | collective-permute-start | bytes 245768 | tf_op jit(solution)/shard_map/ppermute | solution.py:566
  14.2 6.7 %collective-permute-start.2 = (bf16[1,160,256]{2,1,0:T(8,128)(2,1)S(1)}, bf16[1,160,256]{2,1,0:T(8,128)(2,1)S(1)}, u32[]{:S(2)}, u32[]{:S(2)}) collective-permute-start(bf16[1,160,256]{2,1,0:T(8,128)(2,1)S(1)} %broadcast_in_dim.37), channel_id=1, source_target_pairs={{0,8},{1,9},{2,10},{3,11},{4,12},{5,13},{6,14},{7,15},{8,16},{9,17... | collective-permute-start | bytes 245768 | tf_op jit(solution)/shard_map/ppermute | solution.py:566
  15.0 17.9 %collective-permute-start.9 = (bf16[4,144,256]{2,1,0:T(8,128)(2,1)S(1)}, bf16[4,144,256]{2,1,0:T(8,128)(2,1)S(1)}, u32[]{:S(2)}, u32[]{:S(2)}) collective-permute-start(bf16[4,144,256]{2,1,0:T(8,128)(2,1)S(1)} %pad_maximum_fusion.2), channel_id=1, source_target_pairs={{0,2},{1,3},{2,0},{3,1},{4,6},{5,7},{6,4},{7,5},{8,10},{9,11},{10,... | collective-permute-start | bytes 884744 | tf_op jit(solution)/shard_map/ppermute | solution.py:566
  20.9 9.6 %collective-permute-start.3 = (bf16[4,160,256]{2,1,0:T(8,128)(2,1)S(1)}, bf16[4,160,256]{2,1,0:T(8,128)(2,1)S(1)}, u32[]{:S(2)}, u32[]{:S(2)}) collective-permute-start(bf16[4,160,256]{2,1,0:T(8,128)(2,1)S(1)} %pad_maximum_fusion), channel_id=1, source_target_pairs={{0,4},{1,5},{2,6},{3,7},{4,0},{5,1},{6,2},{7,3},{8,12},{9,13},{10,... | collective-permute-start | bytes 983048 | tf_op jit(solution)/shard_map/ppermute | solution.py:566
  31.3 15.7 %collective-permute-start.4 = (bf16[8,160,256]{2,1,0:T(8,128)(2,1)S(1)}, bf16[8,160,256]{2,1,0:T(8,128)(2,1)S(1)}, u32[]{:S(2)}, u32[]{:S(2)}) collective-permute-start(bf16[8,160,256]{2,1,0:T(8,128)(2,1)S(1)} %get-tuple-element.47), channel_id=1, source_target_pairs={{0,2},{1,3},{2,0},{3,1},{4,6},{5,7},{6,4},{7,5},{8,10},{9,11},{10,... | collective-permute-start | bytes 1966088 | tf_op jit(solution)/shard_map/ppermute | solution.py:566
  33.6 16.4 %copy-start.7 = (f32[2,2,384,6]{2,1,3,0:T(2,128)S(1)}, f32[2,2,384,6]{2,1,3,0:T(2,128)}, u32[]{:S(2)}) copy-start(f32[2,2,384,6]{2,1,3,0:T(2,128)} %param.13) | copy-start | bytes 110596
  33.6 14.4 %collective-permute-start.10 = (bf16[8,144,256]{2,1,0:T(8,128)(2,1)S(1)}, bf16[8,144,256]{2,1,0:T(8,128)(2,1)S(1)}, u32[]{:S(2)}, u32[]{:S(2)}) collective-permute-start(bf16[8,144,256]{2,1,0:T(8,128)(2,1)S(1)} %get-tuple-element.49), channel_id=1, source_target_pairs={{0,4},{1,5},{2,6},{3,7},{4,0},{5,1},{6,2},{7,3},{8,12},{9,13},{10,... | collective-permute-start | bytes 1769480 | tf_op jit(solution)/shard_map/ppermute | solution.py:566
  48.0 2.4 %copy-start.11 = (s32[2,2]{1,0:T(2,128)S(1)}, s32[2,2]{1,0:T(2,128)}, u32[]{:S(2)}) copy-start(s32[2,2]{1,0:T(2,128)} %param.15) | copy-start | bytes 52
  48.0 2.5 %copy-start.8 = (f32[2,2,384,6]{2,1,3,0:T(2,128)S(1)}, f32[2,2,384,6]{2,1,3,0:T(2,128)}, u32[]{:S(2)}) copy-start(f32[2,2,384,6]{2,1,3,0:T(2,128)} %param.12) | copy-start | bytes 110596
  48.0 7.4 %collective-permute-start.5 = (bf16[16,160,256]{2,1,0:T(8,128)(2,1)}, bf16[16,160,256]{2,1,0:T(8,128)(2,1)}, u32[]{:S(2)}, u32[]{:S(2)}) collective-permute-start(bf16[16,160,256]{2,1,0:T(8,128)(2,1)} %constant_dynamic-update-slice_fusion.5.a0), channel_id=1, source_target_pairs={{0,1},{1,0},{2,3},{3,2},{4,5},{5,4},{6,7},{7,6},{8,9},{9,8},{10,11... | collective-permute-start | bytes 3932168 | tf_op jit(solution)/shard_map/ppermute | solution.py:566
  48.8 6.5 %collective-permute-start.11 = (bf16[16,144,256]{2,1,0:T(8,128)(2,1)}, bf16[16,144,256]{2,1,0:T(8,128)(2,1)}, u32[]{:S(2)}, u32[]{:S(2)}) collective-permute-start(bf16[16,144,256]{2,1,0:T(8,128)(2,1)} %constant_dynamic-update-slice_fusion.16.b0), channel_id=1, source_target_pairs={{0,1},{1,0},{2,3},{3,2},{4,5},{5,4},{6,7},{7,6},{8,9},{9,8},{10,11... | collective-permute-start | bytes 3538952 | tf_op jit(solution)/shard_map/ppermute | solution.py:566
  50.4 1.6 copy-start.12
  117.9 7.1 %copy-start = (bf16[16,160,256]{2,1,0:T(8,128)(2,1)S(1)}, bf16[16,160,256]{2,1,0:T(8,128)(2,1)}, u32[]{:S(2)}) copy-start(bf16[16,160,256]{2,1,0:T(8,128)(2,1)} %get-tuple-element.13) | copy-start | bytes 3932164
  117.9 3.1 %collective-permute-start.18 = (bf16[16,144,256]{2,1,0:T(8,128)(2,1)}, bf16[16,144,256]{2,1,0:T(8,128)(2,1)S(1)}, u32[]{:S(2)}, u32[]{:S(2)}) collective-permute-start(bf16[16,144,256]{2,1,0:T(8,128)(2,1)} %get-tuple-element.16), channel_id=1, source_target_pairs={{0,1},{1,0},{2,3},{3,2},{4,5},{5,4},{6,7},{7,6},{8,9},{9,8},{10,11... | collective-permute-start | bytes 3538952 | tf_op jit(solution)/shard_map/ppermute | solution.py:566
  118.0 7.0 %collective-permute-start.12 = (bf16[16,160,256]{2,1,0:T(8,128)(2,1)}, bf16[16,160,256]{2,1,0:T(8,128)(2,1)S(1)}, u32[]{:S(2)}, u32[]{:S(2)}) collective-permute-start(bf16[16,160,256]{2,1,0:T(8,128)(2,1)} %get-tuple-element.14), channel_id=1, source_target_pairs={{0,1},{1,0},{2,3},{3,2},{4,5},{5,4},{6,7},{7,6},{8,9},{9,8},{10,11... | collective-permute-start | bytes 3932168 | tf_op jit(solution)/shard_map/ppermute | solution.py:566
  121.0 4.0 %copy-start.3 = (bf16[16,144,256]{2,1,0:T(8,128)(2,1)}, bf16[16,144,256]{2,1,0:T(8,128)(2,1)S(1)}, u32[]{:S(2)}) copy-start(bf16[16,144,256]{2,1,0:T(8,128)(2,1)S(1)} %collective-permute-done.18) | copy-start | bytes 3538948
  123.4 5.3 %copy-start.9 = (f32[8,8]{1,0:T(8,128)S(1)}, f32[8,8]{1,0:T(8,128)}, u32[]{:S(2)}) copy-start(f32[8,8]{1,0:T(8,128)} %get-tuple-element.17) | copy-start | bytes 772
  123.4 15.7 %collective-permute-start.19 = (bf16[8,144,256]{2,1,0:T(8,128)(2,1)}, bf16[8,144,256]{2,1,0:T(8,128)(2,1)}, u32[]{:S(2)}, u32[]{:S(2)}) collective-permute-start(bf16[8,144,256]{2,1,0:T(8,128)(2,1)} %add_convert_fusion.1), channel_id=1, source_target_pairs={{0,4},{1,5},{2,6},{3,7},{4,0},{5,1},{6,2},{7,3},{8,12},{9,13},{10,... | collective-permute-start | bytes 1769480 | tf_op jit(solution)/shard_map/ppermute | solution.py:566
  126.0 17.0 %collective-permute-start.13 = (bf16[8,160,256]{2,1,0:T(8,128)(2,1)}, bf16[8,160,256]{2,1,0:T(8,128)(2,1)S(1)}, u32[]{:S(2)}, u32[]{:S(2)}) collective-permute-start(bf16[8,160,256]{2,1,0:T(8,128)(2,1)} %add_convert_fusion), channel_id=1, source_target_pairs={{0,2},{1,3},{2,0},{3,1},{4,6},{5,7},{6,4},{7,5},{8,10},{9,11},{10,... | collective-permute-start | bytes 1966088 | tf_op jit(solution)/shard_map/ppermute | solution.py:566
  130.0 13.6 %collective-permute-start.24 = (f32[8,128]{1,0:T(8,128)S(1)}, f32[8,128]{1,0:T(8,128)S(1)}, u32[]{:S(2)}, u32[]{:S(2)}) collective-permute-start(f32[8,128]{1,0:T(8,128)S(1)} %broadcast_in_dim.42), channel_id=1, source_target_pairs={{0,1},{1,0},{2,3},{3,2},{4,5},{5,4},{6,7},{7,6},{8,9},{9,8},{10,11... | collective-permute-start | bytes 12296 | tf_op jit(solution)/shard_map/ppermute | solution.py:566
  140.4 8.7 %collective-permute-start.20 = (bf16[4,144,256]{2,1,0:T(8,128)(2,1)S(1)}, bf16[4,144,256]{2,1,0:T(8,128)(2,1)S(1)}, u32[]{:S(2)}, u32[]{:S(2)}) collective-permute-start(bf16[4,144,256]{2,1,0:T(8,128)(2,1)S(1)} %add_convert_fusion.3), channel_id=1, source_target_pairs={{0,2},{1,3},{2,0},{3,1},{4,6},{5,7},{6,4},{7,5},{8,10},{9,11},{10,... | collective-permute-start | bytes 884744 | tf_op jit(solution)/shard_map/ppermute | solution.py:566
  143.0 11.4 %copy-start.4 = (bf16[8,160,256]{2,1,0:T(8,128)(2,1)}, bf16[8,160,256]{2,1,0:T(8,128)(2,1)S(1)}, u32[]{:S(2)}) copy-start(bf16[8,160,256]{2,1,0:T(8,128)(2,1)S(1)} %collective-permute-done.13) | copy-start | bytes 1966084
  143.1 11.1 %collective-permute-start.14 = (bf16[4,160,256]{2,1,0:T(8,128)(2,1)S(1)}, bf16[4,160,256]{2,1,0:T(8,128)(2,1)S(1)}, u32[]{:S(2)}, u32[]{:S(2)}) collective-permute-start(bf16[4,160,256]{2,1,0:T(8,128)(2,1)S(1)} %add_convert_fusion.2), channel_id=1, source_target_pairs={{0,4},{1,5},{2,6},{3,7},{4,0},{5,1},{6,2},{7,3},{8,12},{9,13},{10,... | collective-permute-start | bytes 983048 | tf_op jit(solution)/shard_map/ppermute | solution.py:566
  143.7 23.8 %collective-permute-start.25 = (f32[8,128]{1,0:T(8,128)S(1)}, f32[8,128]{1,0:T(8,128)S(1)}, u32[]{:S(2)}, u32[]{:S(2)}) collective-permute-start(f32[8,128]{1,0:T(8,128)S(1)} %broadcast_add_fusion.1), channel_id=1, source_target_pairs={{0,2},{1,3},{2,0},{3,1},{4,6},{5,7},{6,4},{7,5},{8,10},{9,11},{10,... | collective-permute-start | bytes 12296 | tf_op jit(solution)/shard_map/ppermute | solution.py:566
  150.3 6.4 %collective-permute-start.21 = (bf16[1,144,256]{2,1,0:T(8,128)(2,1)S(1)}, bf16[1,144,256]{2,1,0:T(8,128)(2,1)S(1)}, u32[]{:S(2)}, u32[]{:S(2)}) collective-permute-start(bf16[1,144,256]{2,1,0:T(8,128)(2,1)S(1)} %get-tuple-element.40), channel_id=1, source_target_pairs={{0,8},{1,9},{2,10},{3,11},{4,12},{5,13},{6,14},{7,15},{8,16},{9,17... | collective-permute-start | bytes 221192 | tf_op jit(solution)/shard_map/ppermute | solution.py:566
  150.4 9.1 %collective-permute-start.22 = (bf16[1,144,256]{2,1,0:T(8,128)(2,1)S(1)}, bf16[1,144,256]{2,1,0:T(8,128)(2,1)S(1)}, u32[]{:S(2)}, u32[]{:S(2)}) collective-permute-start(bf16[1,144,256]{2,1,0:T(8,128)(2,1)S(1)} %get-tuple-element.42), channel_id=1, source_target_pairs={{0,16},{1,17},{2,18},{3,19},{4,20},{5,21},{6,22},{7,23},{8,24},{9,... | collective-permute-start | bytes 221192 | tf_op jit(solution)/shard_map/ppermute | solution.py:566
  150.9 11.1 %collective-permute-start.23 = (bf16[1,144,256]{2,1,0:T(8,128)(2,1)S(1)}, bf16[1,144,256]{2,1,0:T(8,128)(2,1)S(1)}, u32[]{:S(2)}, u32[]{:S(2)}) collective-permute-start(bf16[1,144,256]{2,1,0:T(8,128)(2,1)S(1)} %get-tuple-element.41), channel_id=1, source_target_pairs={{0,24},{1,25},{2,26},{3,27},{4,28},{5,29},{6,30},{7,31},{8,0},{9,1... | collective-permute-start | bytes 221192 | tf_op jit(solution)/shard_map/ppermute | solution.py:566
  154.4 8.7 %collective-permute-start.15 = (bf16[1,160,256]{2,1,0:T(8,128)(2,1)S(1)}, bf16[1,160,256]{2,1,0:T(8,128)(2,1)S(1)}, u32[]{:S(2)}, u32[]{:S(2)}) collective-permute-start(bf16[1,160,256]{2,1,0:T(8,128)(2,1)S(1)} %get-tuple-element.37), channel_id=1, source_target_pairs={{0,8},{1,9},{2,10},{3,11},{4,12},{5,13},{6,14},{7,15},{8,16},{9,17... | collective-permute-start | bytes 245768 | tf_op jit(solution)/shard_map/ppermute | solution.py:566
  156.8 8.3 %collective-permute-start.16 = (bf16[1,160,256]{2,1,0:T(8,128)(2,1)S(1)}, bf16[1,160,256]{2,1,0:T(8,128)(2,1)S(1)}, u32[]{:S(2)}, u32[]{:S(2)}) collective-permute-start(bf16[1,160,256]{2,1,0:T(8,128)(2,1)S(1)} %get-tuple-element.39), channel_id=1, source_target_pairs={{0,16},{1,17},{2,18},{3,19},{4,20},{5,21},{6,22},{7,23},{8,24},{9,... | collective-permute-start | bytes 245768 | tf_op jit(solution)/shard_map/ppermute | solution.py:566
  159.5 5.6 %collective-permute-start.17 = (bf16[1,160,256]{2,1,0:T(8,128)(2,1)S(1)}, bf16[1,160,256]{2,1,0:T(8,128)(2,1)S(1)}, u32[]{:S(2)}, u32[]{:S(2)}) collective-permute-start(bf16[1,160,256]{2,1,0:T(8,128)(2,1)S(1)} %get-tuple-element.38), channel_id=1, source_target_pairs={{0,24},{1,25},{2,26},{3,27},{4,28},{5,29},{6,30},{7,31},{8,0},{9,1... | collective-permute-start | bytes 245768 | tf_op jit(solution)/shard_map/ppermute | solution.py:566
  163.0 25.7 %copy-start.1 = (f32[77312]{0:T(1024)S(1)}, f32[77312]{0:T(1024)}, u32[]{:S(2)}) copy-start(f32[77312]{0:T(1024)} %param.8) | copy-start | bytes 927748
  163.0 25.7 %copy-start.5 = (f32[77312]{0:T(1024)S(1)}, f32[77312]{0:T(1024)}, u32[]{:S(2)}) copy-start(f32[77312]{0:T(1024)} %param.9) | copy-start | bytes 927748
  167.4 1.2 collective-permute-start.30
  167.5 3.7 %collective-permute-start.26 = (f32[8,128]{1,0:T(8,128)S(1)}, f32[8,128]{1,0:T(8,128)S(1)}, u32[]{:S(2)}, u32[]{:S(2)}) collective-permute-start(f32[8,128]{1,0:T(8,128)S(1)} %fusion.65), channel_id=1, source_target_pairs={{0,4},{1,5},{2,6},{3,7},{4,0},{5,1},{6,2},{7,3},{8,12},{9,13},{10,... | collective-permute-start | bytes 12296 | tf_op jit(solution)/shard_map/ppermute | solution.py:566
  169.3 6.2 %collective-permute-start.31 = (f32[8,128]{1,0:T(8,128)S(1)}, f32[8,128]{1,0:T(8,128)S(1)}, u32[]{:S(2)}, u32[]{:S(2)}) collective-permute-start(f32[8,128]{1,0:T(8,128)S(1)} %broadcast_add_fusion), channel_id=1, source_target_pairs={{0,2},{1,3},{2,0},{3,1},{4,6},{5,7},{6,4},{7,5},{8,10},{9,11},{10,... | collective-permute-start | bytes 12296 | tf_op jit(solution)/shard_map/ppermute | solution.py:566
  171.1 5.9 %collective-permute-start.27 = (f32[8,128]{1,0:T(8,128)S(1)}, f32[8,128]{1,0:T(8,128)S(1)}, u32[]{:S(2)}, u32[]{:S(2)}) collective-permute-start(f32[8,128]{1,0:T(8,128)S(1)} %add.1037), channel_id=1, source_target_pairs={{0,16},{1,17},{2,18},{3,19},{4,20},{5,21},{6,22},{7,23},{8,24},{9,... | collective-permute-start | bytes 12296 | tf_op jit(solution)/shard_map/ppermute | solution.py:566
  171.7 5.4 %collective-permute-start.28 = (f32[8,128]{1,0:T(8,128)S(1)}, f32[8,128]{1,0:T(8,128)S(1)}, u32[]{:S(2)}, u32[]{:S(2)}) collective-permute-start(f32[8,128]{1,0:T(8,128)S(1)} %add.1037), channel_id=1, source_target_pairs={{0,8},{1,9},{2,10},{3,11},{4,12},{5,13},{6,14},{7,15},{8,16},{9,17... | collective-permute-start | bytes 12296 | tf_op jit(solution)/shard_map/ppermute | solution.py:566
  174.9 3.6 %collective-permute-start.29 = (f32[8,128]{1,0:T(8,128)S(1)}, f32[8,128]{1,0:T(8,128)S(1)}, u32[]{:S(2)}, u32[]{:S(2)}) collective-permute-start(f32[8,128]{1,0:T(8,128)S(1)} %add.1037), channel_id=1, source_target_pairs={{0,24},{1,25},{2,26},{3,27},{4,28},{5,29},{6,30},{7,31},{8,0},{9,1... | collective-permute-start | bytes 12296 | tf_op jit(solution)/shard_map/ppermute | solution.py:566
  176.1 3.7 %collective-permute-start.32 = (f32[8,128]{1,0:T(8,128)S(1)}, f32[8,128]{1,0:T(8,128)S(1)}, u32[]{:S(2)}, u32[]{:S(2)}) collective-permute-start(f32[8,128]{1,0:T(8,128)S(1)} %fusion.66), channel_id=1, source_target_pairs={{0,4},{1,5},{2,6},{3,7},{4,0},{5,1},{6,2},{7,3},{8,12},{9,13},{10,... | collective-permute-start | bytes 12296 | tf_op jit(solution)/shard_map/ppermute | solution.py:566
  179.8 5.3 %collective-permute-start.33 = (f32[8,128]{1,0:T(8,128)S(1)}, f32[8,128]{1,0:T(8,128)S(1)}, u32[]{:S(2)}, u32[]{:S(2)}) collective-permute-start(f32[8,128]{1,0:T(8,128)S(1)} %add.1043), channel_id=1, source_target_pairs={{0,16},{1,17},{2,18},{3,19},{4,20},{5,21},{6,22},{7,23},{8,24},{9,... | collective-permute-start | bytes 12296 | tf_op jit(solution)/shard_map/ppermute | solution.py:566
  180.7 5.4 %collective-permute-start.34 = (f32[8,128]{1,0:T(8,128)S(1)}, f32[8,128]{1,0:T(8,128)S(1)}, u32[]{:S(2)}, u32[]{:S(2)}) collective-permute-start(f32[8,128]{1,0:T(8,128)S(1)} %add.1043), channel_id=1, source_target_pairs={{0,8},{1,9},{2,10},{3,11},{4,12},{5,13},{6,14},{7,15},{8,16},{9,17... | collective-permute-start | bytes 12296 | tf_op jit(solution)/shard_map/ppermute | solution.py:566
  182.0 4.1 %collective-permute-start.35 = (f32[8,128]{1,0:T(8,128)S(1)}, f32[8,128]{1,0:T(8,128)S(1)}, u32[]{:S(2)}, u32[]{:S(2)}) collective-permute-start(f32[8,128]{1,0:T(8,128)S(1)} %add.1043), channel_id=1, source_target_pairs={{0,24},{1,25},{2,26},{3,27},{4,28},{5,29},{6,30},{7,31},{8,0},{9,1... | collective-permute-start | bytes 12296 | tf_op jit(solution)/shard_map/ppermute | solution.py:566
  188.8 2.0 %copy-start.6 = (f32[77312]{0:T(1024)S(1)}, f32[77312]{0:T(1024)}, u32[]{:S(2)}) copy-start(f32[77312]{0:T(1024)} %param.11) | copy-start | bytes 927748
  (1 other events, 0.8 us)
